TPU v7x, 32 devices: a whole 2x2x4 slice. The times are simulated.
32 devices in a mesh: fsdp: 32 (over z, y, x, core).
Axes of the slice: x: 2, y: 2, z: 4, core: 2. Of those that a mesh axis runs over, the one named last changes fastest.
Arguments:
- inputs: bfloat16 [2, 4096, 1280], P(None, 'fsdp'), may hold values from -6 to 6
- cotangent: bfloat16 [2, 4096, 1280], P(None, 'fsdp'), may hold values from -6 to 6
- lengths: int32 [2, 4], replicated, may hold values from 512 to 1024, as said below
- first_gain: float32 [1280], P('fsdp'), may hold values from 0.25 to 1.75
- first_shift: float32 [1280], P('fsdp'), may hold values from -3 to 3
- query_weight: float32 [1280, 1280], P('fsdp'), may hold values from -0.15625 to 0.15625
- query_bias: float32 [1280], P('fsdp'), may hold values from -3 to 3
- key_weight: float32 [1280, 1280], P('fsdp'), may hold values from -0.15625 to 0.15625
- value_weight: float32 [1280, 1280], P('fsdp'), may hold values from -0.15625 to 0.15625
- value_bias: float32 [1280], P('fsdp'), may hold values from -3 to 3
- output_weight: float32 [1280, 1280], P('fsdp'), may hold values from -1.25 to 1.25
- output_bias: float32 [1280], P('fsdp'), may hold values from -3 to 3
- second_gain: float32 [1280], P('fsdp'), may hold values from 0.25 to 1.75
- second_shift: float32 [1280], P('fsdp'), may hold values from -3 to 3
- expand_weight: float32 [1280, 5120], P('fsdp'), may hold values from -0.15625 to 0.15625
- expand_bias: float32 [5120], P('fsdp'), may hold values from -3 to 3
- shrink_weight: float32 [5120, 1280], P('fsdp'), may hold values from -0.078125 to 0.078125
- shrink_bias: float32 [1280], P('fsdp'), may hold values from -3 to 3
Outputs:
- block_out: bfloat16 [2, 4096, 1280], P(None, 'fsdp')
- input_grad: bfloat16 [2, 4096, 1280], P(None, 'fsdp')
- grad_first_gain: float32 [1280], P('fsdp')
- grad_first_shift: float32 [1280], P('fsdp')
- grad_query_weight: float32 [1280, 1280], P('fsdp')
- grad_query_bias: float32 [1280], P('fsdp')
- grad_key_weight: float32 [1280, 1280], P('fsdp')
- grad_value_weight: float32 [1280, 1280], P('fsdp')
- grad_value_bias: float32 [1280], P('fsdp')
- grad_output_weight: float32 [1280, 1280], P('fsdp')
- grad_output_bias: float32 [1280], P('fsdp')
- grad_second_gain: float32 [1280], P('fsdp')
- grad_second_shift: float32 [1280], P('fsdp')
- grad_expand_weight: float32 [1280, 5120], P('fsdp')
- grad_expand_bias: float32 [5120], P('fsdp')
- grad_shrink_weight: float32 [5120, 1280], P('fsdp')
- grad_shrink_bias: float32 [1280], P('fsdp')
Inputs may be any that keep to these rules, and one draw needn't show every extreme that they name: `lengths`: in every micro-batch some clip has all 1024 positions valid.
All inputs are finite; a program needn't handle non-finite values.
Results may differ from a plain program's by a relative error of at most 0.014.
Values may be sent and summed in bfloat16 or wider, within the bound.
A program may use at most 512 MiB of HBM per device.

v0:
```python
from functools import partial

import jax
import jax.numpy as jnp
from jax import lax
from jax.sharding import PartitionSpec as P

H = 16
HD = 80
DEV_CLIP = 8


EPS = 1e-05
NEG = -1000000000.0


def shifted(x, axis, by):
    count = lax.axis_size(axis)
    pairs = [(i, i + by) for i in range(count) if 0 <= i + by < count]
    return lax.ppermute(x, axis, pairs)


def norm_forward(row_block, gain_vec, shift_vec):
    row_mean = jnp.mean(row_block, -1, keepdims=True)
    centered = row_block - row_mean
    inverse = lax.rsqrt(jnp.mean(centered * centered, -1, keepdims=True) + EPS)
    normed = centered * inverse
    return (normed * gain_vec + shift_vec, normed, inverse)


def norm_backward(gradient, normed, inverse, gain_vec):
    scaled = gradient * gain_vec
    return inverse * (
        scaled
        - jnp.mean(scaled, -1, keepdims=True)
        - normed * jnp.mean(scaled * normed, -1, keepdims=True)
    )


def exact_gelu(values_in):
    return jax.nn.gelu(values_in, approximate=False)


def times_plain(left_rows, right_rows):
    return jnp.dot(left_rows, right_rows, preferred_element_type=jnp.float32)


def times_transposed(left_rows, right_rows):
    return lax.dot_general(
        left_rows, right_rows, (((1,), (1,)), ((), ())), preferred_element_type=jnp.float32
    )


def outer_sum(left_rows, right_rows):
    return lax.dot_general(
        left_rows, right_rows, (((0,), (0,)), ((), ())), preferred_element_type=jnp.float32
    )


def split_heads(row_block, groups):
    return row_block.reshape(row_block.shape[0], groups, -1, HD).transpose(1, 0, 2, 3)


def merge_heads(head_parts):
    return head_parts.transpose(1, 0, 2, 3).reshape(head_parts.shape[1], -1)


def head_scores(queries, key_heads, key_valid):
    scores = jnp.einsum(
        "qhd,khd->hqk", queries, key_heads, preferred_element_type=jnp.float32
    ) * HD ** (-0.5)
    return jnp.where(key_valid[None, None, :], scores, NEG)


def attend_forward(block_parts, key_valid):
    queries, key_heads, value_heads = block_parts
    scores = head_scores(queries, key_heads, key_valid)
    row_peak = jnp.max(scores, -1, keepdims=True)
    exponent = jnp.exp(scores - row_peak)
    row_total = jnp.sum(exponent, -1, keepdims=True)
    soft_probs = (exponent / row_total).astype(jnp.bfloat16)
    mixed_heads = jnp.einsum(
        "hqk,khd->qhd", soft_probs, value_heads, preferred_element_type=jnp.float32
    )
    return (mixed_heads, row_peak, row_total)


def attend_backward(block_parts, key_valid):
    queries, key_heads, value_heads, grad_mixed, row_peak, row_total = block_parts
    soft_probs = jnp.exp(head_scores(queries, key_heads, key_valid) - row_peak) / row_total
    grad_probs = jnp.einsum(
        "qhd,khd->hqk", grad_mixed, value_heads, preferred_element_type=jnp.float32
    )
    grad_values = jnp.einsum(
        "hqk,qhd->khd",
        soft_probs.astype(jnp.bfloat16),
        grad_mixed,
        preferred_element_type=jnp.float32,
    )
    inner_sum = jnp.sum(soft_probs * grad_probs, -1, keepdims=True)
    grad_scores = (soft_probs * (grad_probs - inner_sum)).astype(jnp.bfloat16)
    grad_queries = jnp.einsum(
        "hqk,khd->qhd", grad_scores, key_heads, preferred_element_type=jnp.float32
    ) * HD ** (-0.5)
    grad_keys = jnp.einsum(
        "hqk,qhd->khd", grad_scores, queries, preferred_element_type=jnp.float32
    ) * HD ** (-0.5)
    return (grad_queries, grad_keys, grad_values)


def add_terms(running, extra):
    if running is None:
        return tuple(extra)
    return tuple((first_term + second_term for first_term, second_term in zip(running, extra)))


def owned_terms(count, kept, block_rows, feature_width):
    (
        first_low,
        grad_queries,
        grad_keys,
        grad_values,
        mixed_low,
        resid_low,
        second_low,
        grad_hidden,
        active,
        grad_out,
    ) = kept
    block_count = count // block_rows

    def rows_of(left_rows, right_rows):
        return outer_sum(left_rows, right_rows).reshape(block_count, -1, feature_width)

    pieces = [
        rows_of(first_low, grad_queries),
        rows_of(first_low, grad_keys),
        rows_of(first_low, grad_values),
        rows_of(mixed_low, resid_low),
        rows_of(second_low, grad_hidden),
        rows_of(active, grad_out),
    ]
    return jnp.concatenate(pieces, 1).reshape(block_count * block_rows, feature_width)


def body(
    inputs,
    cotangent,
    lengths,
    first_gain,
    first_shift,
    query_weight,
    query_bias,
    key_weight,
    value_weight,
    value_bias,
    output_weight,
    output_bias,
    second_gain,
    second_shift,
    expand_weight,
    expand_bias,
    shrink_weight,
    shrink_bias,
):
    (
        gain_one,
        shift_one,
        bias_query,
        bias_value,
        bias_output,
        gain_two,
        shift_two,
        bias_expand,
        bias_shrink,
    ) = (
        lax.all_gather(first_gain, "fsdp", axis=0, tiled=True),
        lax.all_gather(first_shift, "fsdp", axis=0, tiled=True),
        lax.all_gather(query_bias, "fsdp", axis=0, tiled=True),
        lax.all_gather(value_bias, "fsdp", axis=0, tiled=True),
        lax.all_gather(output_bias, "fsdp", axis=0, tiled=True),
        lax.all_gather(second_gain, "fsdp", axis=0, tiled=True),
        lax.all_gather(second_shift, "fsdp", axis=0, tiled=True),
        lax.all_gather(expand_bias, "fsdp", axis=0, tiled=True),
        lax.all_gather(shrink_bias, "fsdp", axis=0, tiled=True),
    )
    device = lax.axis_index("fsdp")
    position = device % DEV_CLIP
    clip_index = device // DEV_CLIP
    groups = H // min(H, 8)
    tok_rows = inputs.shape[1]
    feature_width = inputs.shape[2]
    ff_width = expand_weight.shape[1]
    share = query_weight.shape[0]
    ff_share = shrink_weight.shape[0]
    ratio = ff_width // feature_width
    block_rows = 4 * share + share * ratio + ff_share
    slot_rows = tok_rows * DEV_CLIP
    key_places = jnp.arange(slot_rows)
    vector_sums = None
    matrix_owned = None
    kept_sets = []
    block_outs = []
    input_grads = []
    for batch_index in range(inputs.shape[0]):
        copies = (
            lax.all_gather(query_weight.astype(jnp.bfloat16), "fsdp", axis=0, tiled=True),
            lax.all_gather(key_weight.astype(jnp.bfloat16), "fsdp", axis=0, tiled=True),
            lax.all_gather(value_weight.astype(jnp.bfloat16), "fsdp", axis=0, tiled=True),
            lax.all_gather(output_weight.astype(jnp.bfloat16), "fsdp", axis=0, tiled=True),
            lax.all_gather(expand_weight.astype(jnp.bfloat16), "fsdp", axis=0, tiled=True),
            lax.all_gather(shrink_weight.astype(jnp.bfloat16), "fsdp", axis=0, tiled=True),
        )
        query_full, key_full, value_full, output_full, expand_full, shrink_full = copies
        clip_length = lax.dynamic_index_in_dim(lengths[batch_index], clip_index, 0, keepdims=False)
        key_valid = key_places < clip_length
        rows_in = inputs[batch_index].astype(jnp.float32)
        first_out, normed_one, inverse_one = norm_forward(rows_in, gain_one, shift_one)
        first_low = first_out.astype(jnp.bfloat16)
        queries = (times_plain(first_low, query_full) + bias_query).astype(jnp.bfloat16)
        key_rows = times_plain(first_low, key_full).astype(jnp.bfloat16)
        values = (times_plain(first_low, value_full) + bias_value).astype(jnp.bfloat16)
        local_pair = jnp.concatenate([key_rows, values], -1)
        lower_parts = []
        upper_parts = []
        for offset in range(1, DEV_CLIP):
            lower_parts.append(shifted(local_pair, "fsdp", offset))
            upper_parts.append(shifted(local_pair, "fsdp", -offset))
        stacked = jnp.stack(lower_parts[::-1] + [local_pair] + upper_parts)
        clip_pair = lax.dynamic_slice_in_dim(stacked, DEV_CLIP - 1 - position, DEV_CLIP, 0).reshape(
            slot_rows, 2 * feature_width
        )
        query_heads = split_heads(queries, groups)
        key_heads = split_heads(clip_pair[:, :feature_width], groups)
        value_heads = split_heads(clip_pair[:, feature_width:], groups)
        head_mixed, row_peak, row_total = lax.map(
            partial(attend_forward, key_valid=key_valid), (query_heads, key_heads, value_heads)
        )
        mixed_low = merge_heads(head_mixed).astype(jnp.bfloat16)
        residual = rows_in + times_plain(mixed_low, output_full) + bias_output
        second_out, normed_two, inverse_two = norm_forward(residual, gain_two, shift_two)
        second_low = second_out.astype(jnp.bfloat16)
        hidden = times_plain(second_low, expand_full) + bias_expand
        active, gelu_back = jax.vjp(exact_gelu, hidden)
        active = active.astype(jnp.bfloat16)
        block_outs.append(
            (residual + times_plain(active, shrink_full) + bias_shrink).astype(jnp.bfloat16)
        )
        copies = (
            lax.all_gather(query_weight.astype(jnp.bfloat16), "fsdp", axis=0, tiled=True),
            lax.all_gather(key_weight.astype(jnp.bfloat16), "fsdp", axis=0, tiled=True),
            lax.all_gather(value_weight.astype(jnp.bfloat16), "fsdp", axis=0, tiled=True),
            lax.all_gather(output_weight.astype(jnp.bfloat16), "fsdp", axis=0, tiled=True),
            lax.all_gather(expand_weight.astype(jnp.bfloat16), "fsdp", axis=0, tiled=True),
            lax.all_gather(shrink_weight.astype(jnp.bfloat16), "fsdp", axis=0, tiled=True),
        )
        query_full, key_full, value_full, output_full, expand_full, shrink_full = copies
        grad_out = cotangent[batch_index]
        grad_rows = grad_out.astype(jnp.float32)
        grad_shrink_b = jnp.sum(grad_rows, 0)
        grad_active = times_transposed(grad_out, shrink_full).astype(jnp.bfloat16)
        grad_hidden = gelu_back(grad_active.astype(jnp.float32))[0].astype(jnp.bfloat16)
        grad_expand_b = jnp.sum(grad_hidden.astype(jnp.float32), 0)
        grad_second = times_transposed(grad_hidden, expand_full)
        grad_gain_two = jnp.sum(grad_second * normed_two, 0)
        grad_shift_two = jnp.sum(grad_second, 0)
        grad_resid = grad_rows + norm_backward(grad_second, normed_two, inverse_two, gain_two)
        resid_low = grad_resid.astype(jnp.bfloat16)
        grad_output_b = jnp.sum(grad_resid, 0)
        grad_mixed = times_transposed(resid_low, output_full).astype(jnp.bfloat16)
        head_gq, head_gk, head_gv = lax.map(
            partial(attend_backward, key_valid=key_valid),
            (
                query_heads,
                key_heads,
                value_heads,
                split_heads(grad_mixed, groups),
                row_peak,
                row_total,
            ),
        )
        grad_queries = merge_heads(head_gq).astype(jnp.bfloat16)
        clip_grads = jnp.concatenate([merge_heads(head_gk), merge_heads(head_gv)], -1).reshape(
            DEV_CLIP, tok_rows, 2 * feature_width
        )
        padded = lax.dynamic_update_slice_in_dim(
            jnp.zeros((2 * DEV_CLIP - 1, tok_rows, 2 * feature_width), jnp.float32),
            clip_grads,
            DEV_CLIP - 1 - position,
            0,
        )
        pair_grads = padded[DEV_CLIP - 1]
        for offset in range(1, DEV_CLIP):
            pair_grads = pair_grads + shifted(
                padded[DEV_CLIP - 1 + offset].astype(jnp.bfloat16), "fsdp", offset
            ).astype(jnp.float32)
            pair_grads = pair_grads + shifted(
                padded[DEV_CLIP - 1 - offset].astype(jnp.bfloat16), "fsdp", -offset
            ).astype(jnp.float32)
        pair_low = pair_grads.astype(jnp.bfloat16)
        grad_keys = pair_low[:, :feature_width]
        grad_values = pair_low[:, feature_width:]
        grad_query_b = jnp.sum(grad_queries.astype(jnp.float32), 0)
        grad_value_b = jnp.sum(grad_values.astype(jnp.float32), 0)
        grad_first = (
            times_transposed(grad_queries, query_full)
            + times_transposed(grad_keys, key_full)
            + times_transposed(grad_values, value_full)
        )
        grad_gain_one = jnp.sum(grad_first * normed_one, 0)
        grad_shift_one = jnp.sum(grad_first, 0)
        input_grads.append(
            (grad_resid + norm_backward(grad_first, normed_one, inverse_one, gain_one)).astype(
                jnp.bfloat16
            )
        )
        vector_sums = add_terms(
            vector_sums,
            (
                grad_gain_one,
                grad_shift_one,
                grad_query_b,
                grad_value_b,
                grad_output_b,
                grad_gain_two,
                grad_shift_two,
                grad_expand_b,
                grad_shrink_b,
            ),
        )
        kept_now = (
            first_low,
            grad_queries,
            grad_keys,
            grad_values,
            mixed_low,
            resid_low,
            second_low,
            grad_hidden,
            active,
            grad_out,
        )
        kept_sets.append(kept_now)
    joined = tuple((jnp.concatenate([kept[item] for kept in kept_sets], 0) for item in range(10)))
    matrix_owned = lax.psum_scatter(
        owned_terms(lax.axis_size("fsdp") * block_rows, joined, block_rows, feature_width),
        "fsdp",
        scatter_dimension=0,
        tiled=True,
    )
    owned_vectors = (
        lax.psum_scatter(vector_sums[0], "fsdp", scatter_dimension=0, tiled=True),
        lax.psum_scatter(vector_sums[1], "fsdp", scatter_dimension=0, tiled=True),
        lax.psum_scatter(vector_sums[2], "fsdp", scatter_dimension=0, tiled=True),
        lax.psum_scatter(vector_sums[3], "fsdp", scatter_dimension=0, tiled=True),
        lax.psum_scatter(vector_sums[4], "fsdp", scatter_dimension=0, tiled=True),
        lax.psum_scatter(vector_sums[5], "fsdp", scatter_dimension=0, tiled=True),
        lax.psum_scatter(vector_sums[6], "fsdp", scatter_dimension=0, tiled=True),
        lax.psum_scatter(vector_sums[7], "fsdp", scatter_dimension=0, tiled=True),
        lax.psum_scatter(vector_sums[8], "fsdp", scatter_dimension=0, tiled=True),
    )
    grad_query_w = matrix_owned[0:share]
    grad_key_w = matrix_owned[share : 2 * share]
    grad_value_w = matrix_owned[2 * share : 3 * share]
    grad_output_w = matrix_owned[3 * share : 4 * share]
    grad_expand_w = matrix_owned[4 * share : 4 * share + share * ratio].reshape(share, ff_width)
    grad_shrink_w = matrix_owned[4 * share + share * ratio :]
    return (
        jnp.stack(block_outs),
        jnp.stack(input_grads),
        owned_vectors[0],
        owned_vectors[1],
        grad_query_w,
        owned_vectors[2],
        grad_key_w,
        grad_value_w,
        owned_vectors[3],
        grad_output_w,
        owned_vectors[4],
        owned_vectors[5],
        owned_vectors[6],
        grad_expand_w,
        owned_vectors[7],
        grad_shrink_w,
        owned_vectors[8],
    )


def solution(mesh):
    in_specs = (
        P(None, "fsdp", None),
        P(None, "fsdp", None),
        P(),
        P("fsdp"),
        P("fsdp"),
        P("fsdp", None),
        P("fsdp"),
        P("fsdp", None),
        P("fsdp", None),
        P("fsdp"),
        P("fsdp", None),
        P("fsdp"),
        P("fsdp"),
        P("fsdp"),
        P("fsdp", None),
        P("fsdp"),
        P("fsdp", None),
        P("fsdp"),
    )
    out_specs = (
        P(None, "fsdp", None),
        P(None, "fsdp", None),
        P("fsdp"),
        P("fsdp"),
        P("fsdp", None),
        P("fsdp"),
        P("fsdp", None),
        P("fsdp", None),
        P("fsdp"),
        P("fsdp", None),
        P("fsdp"),
        P("fsdp"),
        P("fsdp"),
        P("fsdp", None),
        P("fsdp"),
        P("fsdp", None),
        P("fsdp"),
    )
    return jax.shard_map(body, mesh=mesh, in_specs=in_specs, out_specs=out_specs, check_vma=False)
```

profile of v0, /device:TPU:0, one launch (start us, length us, event | category | flops | bytes accessed | tf_op | source)
XLA Modules:
  0.0 2052.2 jit_solution(6773685793462343536)
XLA Ops:
  23.3 44.1 %all-reduce.19 = (f32[1280]{0:T(1024)S(1)}, f32[1280]{0:T(1024)S(1)}, f32[1280]{0:T(1024)S(1)}, f32[1280]{0:T(1024)S(1)}, f32[1280]{0:T(1024)S(1)}, /*index=5*/f...) all-reduce(f32[1280]{0:T(1024)S(1)} %dynamic-update-slice.1, ...), channel_id=1, replica_groups=mesh['fsdp'=32] {'fsdp'}, use_global_device_ids=true, to_apply=%add.1 | all-reduce | flops 14080 | bytes 112640
  68.4 5.4 all-gather.7.cloned.1.call-done
  76.5 59.1 %all-gather.9.cloned.1.call-done = bf16[1280,1280]{1,0:T(8,128)(2,1)} async-done(((bf16[40,1280]{1,0:T(8,128)(2,1)}), bf16[1280,1280]{1,0:T(8,128)(2,1)}) %all-gather.9.cloned.1.call-update) | async-done | bytes 3276816 | tf_op jit(solution)/shard_map/all_gather | solution.py:209
  152.4 4.4 collective-permute-start.18
  156.8 70.8 %all-gather.11.cloned.1.call-done = bf16[1280,1280]{1,0:T(8,128)(2,1)} async-done(((bf16[40,1280]{1,0:T(8,128)(2,1)}), bf16[1280,1280]{1,0:T(8,128)(2,1)}) %all-gather.11.cloned.1.call-update) | async-done | bytes 3276816 | tf_op jit(solution)/shard_map/all_gather | solution.py:207
  255.0 16.5 collective-permute-done.19
  275.7 13.2 collective-permute-done.22
  290.2 9.8 collective-permute-done.23
  303.0 41.0 %collective-permute-start.1 = (bf16[128,2560]{1,0:T(8,128)(2,1)}, bf16[128,2560]{1,0:T(8,128)(2,1)S(1)}, u32[]{:S(2)}, u32[]{:S(2)}) collective-permute-start(bf16[128,2560]{1,0:T(8,128)(2,1)} %pad_maximum_fusion.2), channel_id=1, source_target_pairs={{0,6},{1,7},{2,8},{3,9},{4,10},{5,11},{6,12},{7,13},{8,14},{9,15},... | collective-permute-start | bytes 1966088 | tf_op jit(solution)/shard_map/ppermute | solution.py:20
  345.5 18.0 collective-permute-start.3
  363.5 15.6 collective-permute-start.4
  381.5 14.2 collective-permute-start.5
  396.6 8.0 collective-permute-start.6
  416.4 4.5 copy.67
  427.7 23.6 %collective-permute-done.8 = bf16[128,2560]{1,0:T(8,128)(2,1)} collective-permute-done((bf16[128,2560]{1,0:T(8,128)(2,1)}, bf16[128,2560]{1,0:T(8,128)(2,1)}, u32[]{:S(2)}, u32[]{:S(2)}) %collective-permute-start.8) | collective-permute-done | bytes 655392 | tf_op jit(solution)/shard_map/ppermute | solution.py:20
  454.6 6.0 collective-permute-done.9
  466.7 28.4 %collective-permute-done.12 = bf16[128,2560]{1,0:T(8,128)(2,1)S(1)} collective-permute-done((bf16[128,2560]{1,0:T(8,128)(2,1)}, bf16[128,2560]{1,0:T(8,128)(2,1)S(1)}, u32[]{:S(2)}, u32[]{:S(2)}) %collective-permute-start.12) | collective-permute-done | bytes 655392 | tf_op jit(solution)/shard_map/ppermute | solution.py:20
  495.9 21.0 %collective-permute-done.13 = bf16[128,2560]{1,0:T(8,128)(2,1)S(1)} collective-permute-done((bf16[128,2560]{1,0:T(8,128)(2,1)}, bf16[128,2560]{1,0:T(8,128)(2,1)S(1)}, u32[]{:S(2)}, u32[]{:S(2)}) %collective-permute-start.13) | collective-permute-done | bytes 655392 | tf_op jit(solution)/shard_map/ppermute | solution.py:20
  529.3 13.2 while.60
  547.5 14.9 while.61
  565.5 11.4 multiply_convert_fusion.2
  576.9 8.8 multiply_convert_fusion.3
  585.8 66.0 %all-gather.17.cloned.1.call-done = bf16[5120,1280]{1,0:T(8,128)(2,1)} async-done(((bf16[160,1280]{1,0:T(8,128)(2,1)}), bf16[5120,1280]{1,0:T(8,128)(2,1)}) %all-gather.17.cloned.1.call-update) | async-done | bytes 13107216 | tf_op jit(solution)/shard_map/all_gather | solution.py:212
  651.8 13.1 convert_reduce_fusion.1
  664.9 10.5 fusion.260
  675.4 11.9 convert_reduce_fusion
  687.3 10.6 multiply_reduce_fusion.2
  709.9 25.2 %while.63 = (s32[]{:T(128)}, bf16[2,128,8,80]{1,3,2,0:T(8,128)(2,1)}, f32[2,1024,8,80]{1,3,2,0:T(8,128)}, f32[2,1024,8,80]{1,3,2,0:T(8,128)}, bf16[2,1024,8,80]{...) while((s32[]{:T(128)}, ...), condition=%wide.region_27.28_spmd.clone, body=%wide.region_25.27_spmd.clone.sunk | while | flops 850083840 | bytes 117677392 | solution.py:271
  740.4 9.3 pad_maximum_fusion.1
  749.7 11.5 copy.73
  761.2 9.6 broadcast.316.clone
  770.8 5.2 constant_dynamic-update-slice_fusion.6
  775.9 7.5 convert.33
  789.0 6.0 collective-permute-start.54
  796.3 6.3 collective-permute-start.52
  812.8 25.0 %while.62 = (s32[]{:T(128)}, bf16[2,128,8,80]{1,3,2,0:T(8,128)(2,1)}, f32[2,1024,8,80]{1,3,2,0:T(8,128)}, f32[2,1024,8,80]{1,3,2,0:T(8,128)}, bf16[2,1024,8,80]{...) while((s32[]{:T(128)}, ...), condition=%wide.region_20.21_spmd.clone, body=%wide.region_18.20_spmd.clone.sunk | while | flops 850083840 | bytes 117677392 | solution.py:271
  843.1 9.2 pad_maximum_fusion
  852.4 11.6 copy.71
  864.1 10.7 fusion.124
  874.8 10.8 fusion.120
  885.6 5.1 collective-permute-start.50
  892.0 7.7 collective-permute-start.48
  899.7 9.2 broadcast.316.clone.1
  909.0 5.2 constant_dynamic-update-slice_fusion.7
  914.2 11.7 convert.32
  927.2 29.5 %reshape.268 = f32[32,160,1280]{2,1,0:T(8,128)} reshape(f32[1280,5120]{1,0:T(8,128)} %fusion.120) | data formatting | bytes 52428800 | tf_op jit(solution)/shard_map/reshape | solution.py:133
  968.0 4.6 collective-permute-start.44
  979.3 25.5 %collective-permute-done.46 = bf16[128,2560]{1,0:T(8,128)(2,1)S(1)} collective-permute-done((bf16[128,2560]{1,0:T(8,128)(2,1)}, bf16[128,2560]{1,0:T(8,128)(2,1)S(1)}, u32[]{:S(2)}, u32[]{:S(2)}) %collective-permute-start.46) | collective-permute-done | bytes 655392 | tf_op jit(solution)/shard_map/ppermute | solution.py:20
  1006.1 5.2 collective-permute-start.40
  1011.3 21.5 %collective-permute-done.44 = bf16[128,2560]{1,0:T(8,128)(2,1)S(1)} collective-permute-done((bf16[128,2560]{1,0:T(8,128)(2,1)S(1)}, bf16[128,2560]{1,0:T(8,128)(2,1)S(1)}, u32[]{:S(2)}, u32[]{:S(2)}) %collective-permute-start.44) | collective-permute-done | bytes 655392 | tf_op jit(solution)/shard_map/ppermute | solution.py:20
  1034.1 5.5 collective-permute-start.38
  1043.7 14.9 collective-permute-start.36
  1060.0 11.3 collective-permute-start.34
  1085.8 27.0 %collective-permute-done.36 = bf16[128,2560]{1,0:T(8,128)(2,1)S(1)} collective-permute-done((bf16[128,2560]{1,0:T(8,128)(2,1)S(1)}, bf16[128,2560]{1,0:T(8,128)(2,1)S(1)}, u32[]{:S(2)}, u32[]{:S(2)}) %collective-permute-start.36) | collective-permute-done | bytes 655392 | tf_op jit(solution)/shard_map/ppermute | solution.py:20
  1114.1 10.6 collective-permute-start.30
  1135.5 11.0 collective-permute-done.30
  1168.6 6.7 constant_dynamic-update-slice_fusion.3
  1175.3 6.2 constant_dynamic-update-slice_fusion.2
  1181.6 9.2 constant_dynamic-update-slice_fusion.1
  1191.1 17.6 constant_dynamic-update-slice_fusion
  1212.8 138.2 %all-reduce.22.cloned.1.call-done = (f32[1280]{0:T(1024)}, f32[1280]{0:T(1024)}, f32[1280]{0:T(1024)}, f32[1280]{0:T(1024)}, f32[1280]{0:T(1024)}, /*index=5*/f3...) async-done(((f32[1280]{0:T(1024)}, f32[1280]{0:T(1024)}, f32[1280]{0:T(1024)}, f32[1280]{0:T(1024)}, f32[1280]{0:T(1024)}, ...) | async-done | bytes 66576
  1362.5 8.1 fusion.148
  1370.6 8.8 fusion.149
  1380.4 659.2 %reduce-scatter.2.cloned.1.call-done = f32[480,1280]{1,0:T(8,128)} async-done(((f32[15360,1280]{1,0:T(8,128)}), f32[480,1280]{1,0:T(8,128)}) %reduce-scatter.2.cloned.1.call-update) | async-done | bytes 2457616 | tf_op jit(solution)/shard_map/reduce_scatter | solution.py:345
  (664 shorter events, 340.9 us)
Async XLA Ops:
  7.2 66.7 %all-gather.7.cloned.1.call-start = ((), (), s32[]{:S(2)}) async-start(), calls=%async_computation.1 | async-start | bytes 3379200 | tf_op jit(solution)/shard_map/all_gather | solution.py:208
  9.0 126.6 %all-gather.9.cloned.1.call-start = ((), (), s32[]{:S(2)}) async-start(), calls=%async_computation.2 | async-start | bytes 3379200 | tf_op jit(solution)/shard_map/all_gather | solution.py:209
  10.6 217.0 %all-gather.11.cloned.1.call-start = ((), (), s32[]{:S(2)}) async-start(), calls=%async_computation.3 | async-start | bytes 3379200 | tf_op jit(solution)/shard_map/all_gather | solution.py:207
  12.3 530.2 %all-gather.13.cloned.1.call-start = ((), (), s32[]{:S(2)}) async-start(), calls=%async_computation.4 | async-start | bytes 3379200 | tf_op jit(solution)/shard_map/all_gather | solution.py:210
  14.0 551.5 %all-gather.15.cloned.1.call-start = ((), (), s32[]{:S(2)}) async-start(), calls=%async_computation.5 | async-start | bytes 13516800 | tf_op jit(solution)/shard_map/all_gather | solution.py:211
  16.1 635.7 %all-gather.17.cloned.1.call-start = ((), (), s32[]{:S(2)}) async-start(), calls=%async_computation.6 | async-start | bytes 13516800 | tf_op jit(solution)/shard_map/all_gather | solution.py:212
  17.0 1333.9 %all-reduce.22.cloned.1.call-start = ((), (), s32[]{:S(2)}) async-start(), calls=%async_computation.8 | async-start | bytes 188416
  139.1 102.6 %collective-permute-start.14 = (bf16[128,2560]{1,0:T(8,128)(2,1)}, bf16[128,2560]{1,0:T(8,128)(2,1)}, u32[]{:S(2)}, u32[]{:S(2)}) collective-permute-start(bf16[128,2560]{1,0:T(8,128)(2,1)} %pad_maximum_fusion.3), channel_id=1, source_target_pairs={{0,7},{1,8},{2,9},{3,10},{4,11},{5,12},{6,13},{7,14},{8,15},{9,16}... | collective-permute-start | bytes 1966088 | tf_op jit(solution)/shard_map/ppermute | solution.py:20
  143.1 101.0 %collective-permute-start.15 = (bf16[128,2560]{1,0:T(8,128)(2,1)}, bf16[128,2560]{1,0:T(8,128)(2,1)}, u32[]{:S(2)}, u32[]{:S(2)}) collective-permute-start(bf16[128,2560]{1,0:T(8,128)(2,1)} %pad_maximum_fusion.3), channel_id=1, source_target_pairs={{0,6},{1,7},{2,8},{3,9},{4,10},{5,11},{6,12},{7,13},{8,14},{9,15},... | collective-permute-start | bytes 1966088 | tf_op jit(solution)/shard_map/ppermute | solution.py:20
  147.6 99.9 %collective-permute-start.16 = (bf16[128,2560]{1,0:T(8,128)(2,1)}, bf16[128,2560]{1,0:T(8,128)(2,1)}, u32[]{:S(2)}, u32[]{:S(2)}) collective-permute-start(bf16[128,2560]{1,0:T(8,128)(2,1)} %pad_maximum_fusion.3), channel_id=1, source_target_pairs={{0,5},{1,6},{2,7},{3,8},{4,9},{5,10},{6,11},{7,12},{8,13},{9,14},{... | collective-permute-start | bytes 1966088 | tf_op jit(solution)/shard_map/ppermute | solution.py:20
  149.8 100.2 %collective-permute-start.17 = (bf16[128,2560]{1,0:T(8,128)(2,1)}, bf16[128,2560]{1,0:T(8,128)(2,1)}, u32[]{:S(2)}, u32[]{:S(2)}) collective-permute-start(bf16[128,2560]{1,0:T(8,128)(2,1)} %pad_maximum_fusion.3), channel_id=1, source_target_pairs={{0,4},{1,5},{2,6},{3,7},{4,8},{5,9},{6,10},{7,11},{8,12},{9,13},{1... | collective-permute-start | bytes 1966088 | tf_op jit(solution)/shard_map/ppermute | solution.py:20
  152.4 100.2 %collective-permute-start.18 = (bf16[128,2560]{1,0:T(8,128)(2,1)}, bf16[128,2560]{1,0:T(8,128)(2,1)}, u32[]{:S(2)}, u32[]{:S(2)}) collective-permute-start(bf16[128,2560]{1,0:T(8,128)(2,1)} %pad_maximum_fusion.3), channel_id=1, source_target_pairs={{0,3},{1,4},{2,5},{3,6},{4,7},{5,8},{6,9},{7,10},{8,11},{9,12},{10... | collective-permute-start | bytes 1966088 | tf_op jit(solution)/shard_map/ppermute | solution.py:20
  241.7 29.9 %collective-permute-start.19 = (bf16[128,2560]{1,0:T(8,128)(2,1)}, bf16[128,2560]{1,0:T(8,128)(2,1)S(1)}, u32[]{:S(2)}, u32[]{:S(2)}) collective-permute-start(bf16[128,2560]{1,0:T(8,128)(2,1)} %pad_maximum_fusion.3), channel_id=1, source_target_pairs={{0,2},{1,3},{2,4},{3,5},{4,6},{5,7},{6,8},{7,9},{8,10},{9,11},{10,... | collective-permute-start | bytes 1966088 | tf_op jit(solution)/shard_map/ppermute | solution.py:20
  244.1 28.7 %collective-permute-start.20 = (bf16[128,2560]{1,0:T(8,128)(2,1)}, bf16[128,2560]{1,0:T(8,128)(2,1)S(1)}, u32[]{:S(2)}, u32[]{:S(2)}) collective-permute-start(bf16[128,2560]{1,0:T(8,128)(2,1)} %pad_maximum_fusion.3), channel_id=1, source_target_pairs={{0,1},{1,2},{2,3},{3,4},{4,5},{5,6},{6,7},{7,8},{8,9},{9,10},{10,1... | collective-permute-start | bytes 1966088 | tf_op jit(solution)/shard_map/ppermute | solution.py:20
  247.5 26.8 %collective-permute-start.21 = (bf16[128,2560]{1,0:T(8,128)(2,1)}, bf16[128,2560]{1,0:T(8,128)(2,1)S(1)}, u32[]{:S(2)}, u32[]{:S(2)}) collective-permute-start(bf16[128,2560]{1,0:T(8,128)(2,1)} %pad_maximum_fusion.3), channel_id=1, source_target_pairs={{1,0},{2,1},{3,2},{4,3},{5,4},{6,5},{7,6},{8,7},{9,8},{10,9},{11,1... | collective-permute-start | bytes 1966088 | tf_op jit(solution)/shard_map/ppermute | solution.py:20
  250.0 38.9 %collective-permute-start.22 = (bf16[128,2560]{1,0:T(8,128)(2,1)}, bf16[128,2560]{1,0:T(8,128)(2,1)S(1)}, u32[]{:S(2)}, u32[]{:S(2)}) collective-permute-start(bf16[128,2560]{1,0:T(8,128)(2,1)} %pad_maximum_fusion.3), channel_id=1, source_target_pairs={{2,0},{3,1},{4,2},{5,3},{6,4},{7,5},{8,6},{9,7},{10,8},{11,9},{12,... | collective-permute-start | bytes 1966088 | tf_op jit(solution)/shard_map/ppermute | solution.py:20
  252.6 47.5 %collective-permute-start.23 = (bf16[128,2560]{1,0:T(8,128)(2,1)}, bf16[128,2560]{1,0:T(8,128)(2,1)S(1)}, u32[]{:S(2)}, u32[]{:S(2)}) collective-permute-start(bf16[128,2560]{1,0:T(8,128)(2,1)} %pad_maximum_fusion.3), channel_id=1, source_target_pairs={{3,0},{4,1},{5,2},{6,3},{7,4},{8,5},{9,6},{10,7},{11,8},{12,9},{13... | collective-permute-start | bytes 1966088 | tf_op jit(solution)/shard_map/ppermute | solution.py:20
  271.5 31.4 %collective-permute-start.24 = (bf16[128,2560]{1,0:T(8,128)(2,1)}, bf16[128,2560]{1,0:T(8,128)(2,1)S(1)}, u32[]{:S(2)}, u32[]{:S(2)}) collective-permute-start(bf16[128,2560]{1,0:T(8,128)(2,1)} %pad_maximum_fusion.3), channel_id=1, source_target_pairs={{4,0},{5,1},{6,2},{7,3},{8,4},{9,5},{10,6},{11,7},{12,8},{13,9},{1... | collective-permute-start | bytes 1966088 | tf_op jit(solution)/shard_map/ppermute | solution.py:20
  272.9 71.2 %collective-permute-start.25 = (bf16[128,2560]{1,0:T(8,128)(2,1)}, bf16[128,2560]{1,0:T(8,128)(2,1)S(1)}, u32[]{:S(2)}, u32[]{:S(2)}) collective-permute-start(bf16[128,2560]{1,0:T(8,128)(2,1)} %pad_maximum_fusion.3), channel_id=1, source_target_pairs={{5,0},{6,1},{7,2},{8,3},{9,4},{10,5},{11,6},{12,7},{13,8},{14,9},{... | collective-permute-start | bytes 1966088 | tf_op jit(solution)/shard_map/ppermute | solution.py:20
  274.3 71.2 %collective-permute-start.26 = (bf16[128,2560]{1,0:T(8,128)(2,1)}, bf16[128,2560]{1,0:T(8,128)(2,1)S(1)}, u32[]{:S(2)}, u32[]{:S(2)}) collective-permute-start(bf16[128,2560]{1,0:T(8,128)(2,1)} %pad_maximum_fusion.3), channel_id=1, source_target_pairs={{6,0},{7,1},{8,2},{9,3},{10,4},{11,5},{12,6},{13,7},{14,8},{15,9},... | collective-permute-start | bytes 1966088 | tf_op jit(solution)/shard_map/ppermute | solution.py:20
  288.8 74.7 %collective-permute-start.27 = (bf16[128,2560]{1,0:T(8,128)(2,1)}, bf16[128,2560]{1,0:T(8,128)(2,1)S(1)}, u32[]{:S(2)}, u32[]{:S(2)}) collective-permute-start(bf16[128,2560]{1,0:T(8,128)(2,1)} %pad_maximum_fusion.3), channel_id=1, source_target_pairs={{7,0},{8,1},{9,2},{10,3},{11,4},{12,5},{13,6},{14,7},{15,8},{16,9}... | collective-permute-start | bytes 1966088 | tf_op jit(solution)/shard_map/ppermute | solution.py:20
  300.0 81.4 %collective-permute-start = (bf16[128,2560]{1,0:T(8,128)(2,1)}, bf16[128,2560]{1,0:T(8,128)(2,1)S(1)}, u32[]{:S(2)}, u32[]{:S(2)}) collective-permute-start(bf16[128,2560]{1,0:T(8,128)(2,1)} %pad_maximum_fusion.2), channel_id=1, source_target_pairs={{0,7},{1,8},{2,9},{3,10},{4,11},{5,12},{6,13},{7,14},{8,15},{9,16}... | collective-permute-start | bytes 1966088 | tf_op jit(solution)/shard_map/ppermute | solution.py:20
  303.0 93.6 %collective-permute-start.1 = (bf16[128,2560]{1,0:T(8,128)(2,1)}, bf16[128,2560]{1,0:T(8,128)(2,1)S(1)}, u32[]{:S(2)}, u32[]{:S(2)}) collective-permute-start(bf16[128,2560]{1,0:T(8,128)(2,1)} %pad_maximum_fusion.2), channel_id=1, source_target_pairs={{0,6},{1,7},{2,8},{3,9},{4,10},{5,11},{6,12},{7,13},{8,14},{9,15},... | collective-permute-start | bytes 1966088 | tf_op jit(solution)/shard_map/ppermute | solution.py:20
  344.1 61.4 %collective-permute-start.2 = (bf16[128,2560]{1,0:T(8,128)(2,1)}, bf16[128,2560]{1,0:T(8,128)(2,1)S(1)}, u32[]{:S(2)}, u32[]{:S(2)}) collective-permute-start(bf16[128,2560]{1,0:T(8,128)(2,1)} %pad_maximum_fusion.2), channel_id=1, source_target_pairs={{0,5},{1,6},{2,7},{3,8},{4,9},{5,10},{6,11},{7,12},{8,13},{9,14},{... | collective-permute-start | bytes 1966088 | tf_op jit(solution)/shard_map/ppermute | solution.py:20
  345.5 62.1 %collective-permute-start.3 = (bf16[128,2560]{1,0:T(8,128)(2,1)}, bf16[128,2560]{1,0:T(8,128)(2,1)S(1)}, u32[]{:S(2)}, u32[]{:S(2)}) collective-permute-start(bf16[128,2560]{1,0:T(8,128)(2,1)} %pad_maximum_fusion.2), channel_id=1, source_target_pairs={{0,4},{1,5},{2,6},{3,7},{4,8},{5,9},{6,10},{7,11},{8,12},{9,13},{1... | collective-permute-start | bytes 1966088 | tf_op jit(solution)/shard_map/ppermute | solution.py:20
  363.5 46.3 %collective-permute-start.4 = (bf16[128,2560]{1,0:T(8,128)(2,1)}, bf16[128,2560]{1,0:T(8,128)(2,1)S(1)}, u32[]{:S(2)}, u32[]{:S(2)}) collective-permute-start(bf16[128,2560]{1,0:T(8,128)(2,1)} %pad_maximum_fusion.2), channel_id=1, source_target_pairs={{0,3},{1,4},{2,5},{3,6},{4,7},{5,8},{6,9},{7,10},{8,11},{9,12},{10... | collective-permute-start | bytes 1966088 | tf_op jit(solution)/shard_map/ppermute | solution.py:20
  381.5 30.6 %collective-permute-start.5 = (bf16[128,2560]{1,0:T(8,128)(2,1)}, bf16[128,2560]{1,0:T(8,128)(2,1)S(1)}, u32[]{:S(2)}, u32[]{:S(2)}) collective-permute-start(bf16[128,2560]{1,0:T(8,128)(2,1)} %pad_maximum_fusion.2), channel_id=1, source_target_pairs={{0,2},{1,3},{2,4},{3,5},{4,6},{5,7},{6,8},{7,9},{8,10},{9,11},{10,... | collective-permute-start | bytes 1966088 | tf_op jit(solution)/shard_map/ppermute | solution.py:20
  396.6 17.6 collective-permute-start.6
  405.4 19.0 collective-permute-start.7
  407.6 43.7 %collective-permute-start.8 = (bf16[128,2560]{1,0:T(8,128)(2,1)}, bf16[128,2560]{1,0:T(8,128)(2,1)}, u32[]{:S(2)}, u32[]{:S(2)}) collective-permute-start(bf16[128,2560]{1,0:T(8,128)(2,1)} %pad_maximum_fusion.2), channel_id=1, source_target_pairs={{2,0},{3,1},{4,2},{5,3},{6,4},{7,5},{8,6},{9,7},{10,8},{11,9},{12,... | collective-permute-start | bytes 1966088 | tf_op jit(solution)/shard_map/ppermute | solution.py:20
  409.8 50.9 %collective-permute-start.9 = (bf16[128,2560]{1,0:T(8,128)(2,1)}, bf16[128,2560]{1,0:T(8,128)(2,1)}, u32[]{:S(2)}, u32[]{:S(2)}) collective-permute-start(bf16[128,2560]{1,0:T(8,128)(2,1)} %pad_maximum_fusion.2), channel_id=1, source_target_pairs={{3,0},{4,1},{5,2},{6,3},{7,4},{8,5},{9,6},{10,7},{11,8},{12,9},{13... | collective-permute-start | bytes 1966088 | tf_op jit(solution)/shard_map/ppermute | solution.py:20
  412.0 50.7 %collective-permute-start.10 = (bf16[128,2560]{1,0:T(8,128)(2,1)}, bf16[128,2560]{1,0:T(8,128)(2,1)}, u32[]{:S(2)}, u32[]{:S(2)}) collective-permute-start(bf16[128,2560]{1,0:T(8,128)(2,1)} %pad_maximum_fusion.2), channel_id=1, source_target_pairs={{4,0},{5,1},{6,2},{7,3},{8,4},{9,5},{10,6},{11,7},{12,8},{13,9},{1... | collective-permute-start | bytes 1966088 | tf_op jit(solution)/shard_map/ppermute | solution.py:20
  414.2 50.5 %collective-permute-start.11 = (bf16[128,2560]{1,0:T(8,128)(2,1)}, bf16[128,2560]{1,0:T(8,128)(2,1)}, u32[]{:S(2)}, u32[]{:S(2)}) collective-permute-start(bf16[128,2560]{1,0:T(8,128)(2,1)} %pad_maximum_fusion.2), channel_id=1, source_target_pairs={{5,0},{6,1},{7,2},{8,3},{9,4},{10,5},{11,6},{12,7},{13,8},{14,9},{... | collective-permute-start | bytes 1966088 | tf_op jit(solution)/shard_map/ppermute | solution.py:20
  424.5 70.6 %collective-permute-start.12 = (bf16[128,2560]{1,0:T(8,128)(2,1)}, bf16[128,2560]{1,0:T(8,128)(2,1)S(1)}, u32[]{:S(2)}, u32[]{:S(2)}) collective-permute-start(bf16[128,2560]{1,0:T(8,128)(2,1)} %pad_maximum_fusion.2), channel_id=1, source_target_pairs={{6,0},{7,1},{8,2},{9,3},{10,4},{11,5},{12,6},{13,7},{14,8},{15,9},... | collective-permute-start | bytes 1966088 | tf_op jit(solution)/shard_map/ppermute | solution.py:20
  451.4 65.5 %collective-permute-start.13 = (bf16[128,2560]{1,0:T(8,128)(2,1)}, bf16[128,2560]{1,0:T(8,128)(2,1)S(1)}, u32[]{:S(2)}, u32[]{:S(2)}) collective-permute-start(bf16[128,2560]{1,0:T(8,128)(2,1)} %pad_maximum_fusion.2), channel_id=1, source_target_pairs={{7,0},{8,1},{9,2},{10,3},{11,4},{12,5},{13,6},{14,7},{15,8},{16,9}... | collective-permute-start | bytes 1966088 | tf_op jit(solution)/shard_map/ppermute | solution.py:20
  787.7 97.9 %collective-permute-start.55 = (bf16[128,2560]{1,0:T(8,128)(2,1)}, bf16[128,2560]{1,0:T(8,128)(2,1)}, u32[]{:S(2)}, u32[]{:S(2)}) collective-permute-start(bf16[128,2560]{1,0:T(8,128)(2,1)} %get-tuple-element.462), channel_id=1, source_target_pairs={{7,0},{8,1},{9,2},{10,3},{11,4},{12,5},{13,6},{14,7},{15,8},{16,9}... | collective-permute-start | bytes 1966088 | tf_op jit(solution)/shard_map/ppermute | solution.py:20
  789.0 101.7 %collective-permute-start.54 = (bf16[128,2560]{1,0:T(8,128)(2,1)}, bf16[128,2560]{1,0:T(8,128)(2,1)}, u32[]{:S(2)}, u32[]{:S(2)}) collective-permute-start(bf16[128,2560]{1,0:T(8,128)(2,1)} %get-tuple-element.463), channel_id=1, source_target_pairs={{0,7},{1,8},{2,9},{3,10},{4,11},{5,12},{6,13},{7,14},{8,15},{9,16}... | collective-permute-start | bytes 1966088 | tf_op jit(solution)/shard_map/ppermute | solution.py:20
  795.1 96.9 %collective-permute-start.53 = (bf16[128,2560]{1,0:T(8,128)(2,1)}, bf16[128,2560]{1,0:T(8,128)(2,1)}, u32[]{:S(2)}, u32[]{:S(2)}) collective-permute-start(bf16[128,2560]{1,0:T(8,128)(2,1)} %get-tuple-element.464), channel_id=1, source_target_pairs={{6,0},{7,1},{8,2},{9,3},{10,4},{11,5},{12,6},{13,7},{14,8},{15,9},... | collective-permute-start | bytes 1966088 | tf_op jit(solution)/shard_map/ppermute | solution.py:20
  796.3 164.4 %collective-permute-start.52 = (bf16[128,2560]{1,0:T(8,128)(2,1)}, bf16[128,2560]{1,0:T(8,128)(2,1)}, u32[]{:S(2)}, u32[]{:S(2)}) collective-permute-start(bf16[128,2560]{1,0:T(8,128)(2,1)} %get-tuple-element.465), channel_id=1, source_target_pairs={{0,6},{1,7},{2,8},{3,9},{4,10},{5,11},{6,12},{7,13},{8,14},{9,15},... | collective-permute-start | bytes 1966088 | tf_op jit(solution)/shard_map/ppermute | solution.py:20
  802.6 159.7 %collective-permute-start.51 = (bf16[128,2560]{1,0:T(8,128)(2,1)}, bf16[128,2560]{1,0:T(8,128)(2,1)}, u32[]{:S(2)}, u32[]{:S(2)}) collective-permute-start(bf16[128,2560]{1,0:T(8,128)(2,1)} %get-tuple-element.466), channel_id=1, source_target_pairs={{5,0},{6,1},{7,2},{8,3},{9,4},{10,5},{11,6},{12,7},{13,8},{14,9},{... | collective-permute-start | bytes 1966088 | tf_op jit(solution)/shard_map/ppermute | solution.py:20
  885.6 81.0 %collective-permute-start.50 = (bf16[128,2560]{1,0:T(8,128)(2,1)}, bf16[128,2560]{1,0:T(8,128)(2,1)}, u32[]{:S(2)}, u32[]{:S(2)}) collective-permute-start(bf16[128,2560]{1,0:T(8,128)(2,1)} %get-tuple-element.467), channel_id=1, source_target_pairs={{0,5},{1,6},{2,7},{3,8},{4,9},{5,10},{6,11},{7,12},{8,13},{9,14},{... | collective-permute-start | bytes 1966088 | tf_op jit(solution)/shard_map/ppermute | solution.py:20
  890.7 77.3 %collective-permute-start.49 = (bf16[128,2560]{1,0:T(8,128)(2,1)}, bf16[128,2560]{1,0:T(8,128)(2,1)}, u32[]{:S(2)}, u32[]{:S(2)}) collective-permute-start(bf16[128,2560]{1,0:T(8,128)(2,1)} %get-tuple-element.468), channel_id=1, source_target_pairs={{4,0},{5,1},{6,2},{7,3},{8,4},{9,5},{10,6},{11,7},{12,8},{13,9},{1... | collective-permute-start | bytes 1966088 | tf_op jit(solution)/shard_map/ppermute | solution.py:20
  892.0 80.6 %collective-permute-start.48 = (bf16[128,2560]{1,0:T(8,128)(2,1)}, bf16[128,2560]{1,0:T(8,128)(2,1)}, u32[]{:S(2)}, u32[]{:S(2)}) collective-permute-start(bf16[128,2560]{1,0:T(8,128)(2,1)} %get-tuple-element.469), channel_id=1, source_target_pairs={{0,4},{1,5},{2,6},{3,7},{4,8},{5,9},{6,10},{7,11},{8,12},{9,13},{1... | collective-permute-start | bytes 1966088 | tf_op jit(solution)/shard_map/ppermute | solution.py:20
  960.7 17.2 collective-permute-start.47
  962.3 42.5 %collective-permute-start.46 = (bf16[128,2560]{1,0:T(8,128)(2,1)}, bf16[128,2560]{1,0:T(8,128)(2,1)S(1)}, u32[]{:S(2)}, u32[]{:S(2)}) collective-permute-start(bf16[128,2560]{1,0:T(8,128)(2,1)} %get-tuple-element.471), channel_id=1, source_target_pairs={{0,3},{1,4},{2,5},{3,6},{4,7},{5,8},{6,9},{7,10},{8,11},{9,12},{10... | collective-permute-start | bytes 1966088 | tf_op jit(solution)/shard_map/ppermute | solution.py:20
  966.6 39.5 %collective-permute-start.45 = (bf16[128,2560]{1,0:T(8,128)(2,1)}, bf16[128,2560]{1,0:T(8,128)(2,1)S(1)}, u32[]{:S(2)}, u32[]{:S(2)}) collective-permute-start(bf16[128,2560]{1,0:T(8,128)(2,1)} %get-tuple-element.472), channel_id=1, source_target_pairs={{2,0},{3,1},{4,2},{5,3},{6,4},{7,5},{8,6},{9,7},{10,8},{11,9},{12,... | collective-permute-start | bytes 1966088 | tf_op jit(solution)/shard_map/ppermute | solution.py:20
  968.0 64.8 %collective-permute-start.44 = (bf16[128,2560]{1,0:T(8,128)(2,1)S(1)}, bf16[128,2560]{1,0:T(8,128)(2,1)S(1)}, u32[]{:S(2)}, u32[]{:S(2)}) collective-permute-start(bf16[128,2560]{1,0:T(8,128)(2,1)S(1)} %copy-done.85), channel_id=1, source_target_pairs={{0,2},{1,3},{2,4},{3,5},{4,6},{5,7},{6,8},{7,9},{8,10},{9,11},{10,... | collective-permute-start | bytes 1966088 | tf_op jit(solution)/shard_map/ppermute | solution.py:20
  972.6 61.5 %collective-permute-start.43 = (bf16[128,2560]{1,0:T(8,128)(2,1)S(1)}, bf16[128,2560]{1,0:T(8,128)(2,1)S(1)}, u32[]{:S(2)}, u32[]{:S(2)}) collective-permute-start(bf16[128,2560]{1,0:T(8,128)(2,1)S(1)} %copy-done.84), channel_id=1, source_target_pairs={{1,0},{2,1},{3,2},{4,3},{5,4},{6,5},{7,6},{8,7},{9,8},{10,9},{11,1... | collective-permute-start | bytes 1966088 | tf_op jit(solution)/shard_map/ppermute | solution.py:20
  977.9 64.1 %collective-permute-start.42 = (bf16[128,2560]{1,0:T(8,128)(2,1)S(1)}, bf16[128,2560]{1,0:T(8,128)(2,1)S(1)}, u32[]{:S(2)}, u32[]{:S(2)}) collective-permute-start(bf16[128,2560]{1,0:T(8,128)(2,1)S(1)} %copy-done.83), channel_id=1, source_target_pairs={{0,1},{1,2},{2,3},{3,4},{4,5},{5,6},{6,7},{7,8},{8,9},{9,10},{10,1... | collective-permute-start | bytes 1966088 | tf_op jit(solution)/shard_map/ppermute | solution.py:20
  1004.8 38.9 %collective-permute-start.41 = (bf16[128,2560]{1,0:T(8,128)(2,1)S(1)}, bf16[128,2560]{1,0:T(8,128)(2,1)S(1)}, u32[]{:S(2)}, u32[]{:S(2)}) collective-permute-start(bf16[128,2560]{1,0:T(8,128)(2,1)S(1)} %get-tuple-element.476), channel_id=1, source_target_pairs={{7,0},{8,1},{9,2},{10,3},{11,4},{12,5},{13,6},{14,7},{15,8},{16,9}... | collective-permute-start | bytes 1966088 | tf_op jit(solution)/shard_map/ppermute | solution.py:20
  1006.1 52.6 %collective-permute-start.40 = (bf16[128,2560]{1,0:T(8,128)(2,1)S(1)}, bf16[128,2560]{1,0:T(8,128)(2,1)S(1)}, u32[]{:S(2)}, u32[]{:S(2)}) collective-permute-start(bf16[128,2560]{1,0:T(8,128)(2,1)S(1)} %get-tuple-element.477), channel_id=1, source_target_pairs={{0,7},{1,8},{2,9},{3,10},{4,11},{5,12},{6,13},{7,14},{8,15},{9,16}... | collective-permute-start | bytes 1966088 | tf_op jit(solution)/shard_map/ppermute | solution.py:20
  1032.8 27.2 %collective-permute-start.39 = (bf16[128,2560]{1,0:T(8,128)(2,1)S(1)}, bf16[128,2560]{1,0:T(8,128)(2,1)S(1)}, u32[]{:S(2)}, u32[]{:S(2)}) collective-permute-start(bf16[128,2560]{1,0:T(8,128)(2,1)S(1)} %get-tuple-element.478), channel_id=1, source_target_pairs={{6,0},{7,1},{8,2},{9,3},{10,4},{11,5},{12,6},{13,7},{14,8},{15,9},... | collective-permute-start | bytes 1966088 | tf_op jit(solution)/shard_map/ppermute | solution.py:20
  1034.1 39.2 %collective-permute-start.38 = (bf16[128,2560]{1,0:T(8,128)(2,1)S(1)}, bf16[128,2560]{1,0:T(8,128)(2,1)S(1)}, u32[]{:S(2)}, u32[]{:S(2)}) collective-permute-start(bf16[128,2560]{1,0:T(8,128)(2,1)S(1)} %get-tuple-element.479), channel_id=1, source_target_pairs={{0,6},{1,7},{2,8},{3,9},{4,10},{5,11},{6,12},{7,13},{8,14},{9,15},... | collective-permute-start | bytes 1966088 | tf_op jit(solution)/shard_map/ppermute | solution.py:20
  1042.0 39.4 %collective-permute-start.37 = (bf16[128,2560]{1,0:T(8,128)(2,1)S(1)}, bf16[128,2560]{1,0:T(8,128)(2,1)S(1)}, u32[]{:S(2)}, u32[]{:S(2)}) collective-permute-start(bf16[128,2560]{1,0:T(8,128)(2,1)S(1)} %get-tuple-element.480), channel_id=1, source_target_pairs={{5,0},{6,1},{7,2},{8,3},{9,4},{10,5},{11,6},{12,7},{13,8},{14,9},{... | collective-permute-start | bytes 1966088 | tf_op jit(solution)/shard_map/ppermute | solution.py:20
  1043.7 69.0 %collective-permute-start.36 = (bf16[128,2560]{1,0:T(8,128)(2,1)S(1)}, bf16[128,2560]{1,0:T(8,128)(2,1)S(1)}, u32[]{:S(2)}, u32[]{:S(2)}) collective-permute-start(bf16[128,2560]{1,0:T(8,128)(2,1)S(1)} %get-tuple-element.481), channel_id=1, source_target_pairs={{0,5},{1,6},{2,7},{3,8},{4,9},{5,10},{6,11},{7,12},{8,13},{9,14},{... | collective-permute-start | bytes 1966088 | tf_op jit(solution)/shard_map/ppermute | solution.py:20
  1058.7 55.4 %collective-permute-start.35 = (bf16[128,2560]{1,0:T(8,128)(2,1)S(1)}, bf16[128,2560]{1,0:T(8,128)(2,1)S(1)}, u32[]{:S(2)}, u32[]{:S(2)}) collective-permute-start(bf16[128,2560]{1,0:T(8,128)(2,1)S(1)} %get-tuple-element.482), channel_id=1, source_target_pairs={{4,0},{5,1},{6,2},{7,3},{8,4},{9,5},{10,6},{11,7},{12,8},{13,9},{1... | collective-permute-start | bytes 1966088 | tf_op jit(solution)/shard_map/ppermute | solution.py:20
  1060.0 66.8 %collective-permute-start.34 = (bf16[128,2560]{1,0:T(8,128)(2,1)S(1)}, bf16[128,2560]{1,0:T(8,128)(2,1)S(1)}, u32[]{:S(2)}, u32[]{:S(2)}) collective-permute-start(bf16[128,2560]{1,0:T(8,128)(2,1)S(1)} %get-tuple-element.483), channel_id=1, source_target_pairs={{0,4},{1,5},{2,6},{3,7},{4,8},{5,9},{6,10},{7,11},{8,12},{9,13},{1... | collective-permute-start | bytes 1966088 | tf_op jit(solution)/shard_map/ppermute | solution.py:20
  1073.3 54.8 %collective-permute-start.33 = (bf16[128,2560]{1,0:T(8,128)(2,1)S(1)}, bf16[128,2560]{1,0:T(8,128)(2,1)S(1)}, u32[]{:S(2)}, u32[]{:S(2)}) collective-permute-start(bf16[128,2560]{1,0:T(8,128)(2,1)S(1)} %get-tuple-element.484), channel_id=1, source_target_pairs={{3,0},{4,1},{5,2},{6,3},{7,4},{8,5},{9,6},{10,7},{11,8},{12,9},{13... | collective-permute-start | bytes 1966088 | tf_op jit(solution)/shard_map/ppermute | solution.py:20
  1081.4 54.1 %collective-permute-start.32 = (bf16[128,2560]{1,0:T(8,128)(2,1)S(1)}, bf16[128,2560]{1,0:T(8,128)(2,1)S(1)}, u32[]{:S(2)}, u32[]{:S(2)}) collective-permute-start(bf16[128,2560]{1,0:T(8,128)(2,1)S(1)} %get-tuple-element.485), channel_id=1, source_target_pairs={{0,3},{1,4},{2,5},{3,6},{4,7},{5,8},{6,9},{7,10},{8,11},{9,12},{10... | collective-permute-start | bytes 1966088 | tf_op jit(solution)/shard_map/ppermute | solution.py:20
  1112.8 22.7 %collective-permute-start.31 = (bf16[128,2560]{1,0:T(8,128)(2,1)S(1)}, bf16[128,2560]{1,0:T(8,128)(2,1)S(1)}, u32[]{:S(2)}, u32[]{:S(2)}) collective-permute-start(bf16[128,2560]{1,0:T(8,128)(2,1)S(1)} %get-tuple-element.486), channel_id=1, source_target_pairs={{2,0},{3,1},{4,2},{5,3},{6,4},{7,5},{8,6},{9,7},{10,8},{11,9},{12,... | collective-permute-start | bytes 1966088 | tf_op jit(solution)/shard_map/ppermute | solution.py:20
  1114.1 32.5 %collective-permute-start.30 = (bf16[128,2560]{1,0:T(8,128)(2,1)S(1)}, bf16[128,2560]{1,0:T(8,128)(2,1)S(1)}, u32[]{:S(2)}, u32[]{:S(2)}) collective-permute-start(bf16[128,2560]{1,0:T(8,128)(2,1)S(1)} %get-tuple-element.487), channel_id=1, source_target_pairs={{0,2},{1,3},{2,4},{3,5},{4,6},{5,7},{6,8},{7,9},{8,10},{9,11},{10,... | collective-permute-start | bytes 1966088 | tf_op jit(solution)/shard_map/ppermute | solution.py:20
  1126.8 19.7 collective-permute-start.29
  1128.1 18.4 collective-permute-start.28
  1190.9 848.7 %reduce-scatter.2.cloned.1.call-start = ((), (), s32[]{:S(2)}) async-start(), calls=%async_computation.7 | async-start | bytes 81100800 | tf_op jit(solution)/shard_map/reduce_scatter | solution.py:345
  (165 other events, 2147.2 us)
Sparse Core Ops, SparseCore 0:
  11.5 62.3 all-gather.6
  77.3 58.2 all-gather.8
  139.0 88.5 all-gather.10
  230.9 100.6 all-gather.12
  334.9 218.5 all-gather.14
  556.2 95.5 all-gather.16
  1191.0 159.8 all-reduce.21
  1358.5 681.0 reduce-scatter.1
where the time goes:
time: 2070 us; the launch traced here: 2050 us
  waiting for transfers between devices  1210 us (58%)
  local copies, waits for them, and re-layouts  261 us (13%)
  starting transfers between devices  250 us (12%)
  matrix products  185 us (9%)
  other arithmetic  84.1 us (4%)
  blocking collectives  44.1 us (2%)
    reduce_scatter x1, waiting for transfers between devices, body(): lax.psum_scatter(owned_terms(lax.axis_size('fsdp') * block_rows, joined,...  659 us
    ppermute x56, starting transfers between devices, shifted(): return lax.ppermute(x, axis, pairs)  250 us
    ppermute x56, waiting for transfers between devices, shifted(): return lax.ppermute(x, axis, pairs)  211 us
    unnamed x9, waiting for transfers between devices  138 us
    unnamed x304, local copies, waits for them, and re-layouts  83.6 us
    all_gather x1, waiting for transfers between devices, body(): lax.all_gather(query_weight.astype(jnp.bfloat16), 'fsdp', axis=0, tiled=T...  70.8 us
    all_gather x1, waiting for transfers between devices, body(): lax.all_gather(shrink_weight.astype(jnp.bfloat16), 'fsdp', axis=0, tiled=...  66 us
    all_gather x1, waiting for transfers between devices, body(): lax.all_gather(value_weight.astype(jnp.bfloat16), 'fsdp', axis=0, tiled=T...  59.1 us
  transfers between devices with their start and end apart: 64, of which 20 were waited for; matrix products, arithmetic and copies ran while one was open for 16% of the time, Pallas kernels for 0%

commit v1 on v0

v1 whole, which is shorter than its diff:
```python
from functools import partial

import jax
import jax.numpy as jnp
from jax import lax
from jax.experimental import pallas as pl
from jax.experimental.pallas import tpu as pltpu
from jax.sharding import PartitionSpec as P

H = 16
HD = 80
CHIPS = 4
CORES = 2
DEV_CLIP = CHIPS * CORES
OWN_HEADS = H // CHIPS
OWN_FEATURES = OWN_HEADS * HD
QKV_WIDTH = 1024
TILE = 256
VEC_ROWS = 16
ROW_GAIN_ONE, ROW_SHIFT_ONE, ROW_GAIN_TWO, ROW_SHIFT_TWO, ROW_BIAS_OUT, ROW_BIAS_SHRINK = range(6)
ROW_EXPAND = 8
ROW_QKV = 12

EPS = 1e-05
NEG = -1000000000.0
SCALE = HD ** (-0.5)
BF = jnp.bfloat16
F32 = jnp.float32


def dot_nn(left, right):
    return lax.dot_general(left, right, (((1,), (0,)), ((), ())), preferred_element_type=F32)


def dot_nt(left, right):
    return lax.dot_general(left, right, (((1,), (1,)), ((), ())), preferred_element_type=F32)


def dot_tn(left, right):
    return lax.dot_general(left, right, (((0,), (0,)), ((), ())), preferred_element_type=F32)


def norm_parts(rows):
    mean = jnp.mean(rows, -1, keepdims=True)
    centered = rows - mean
    inverse = lax.rsqrt(jnp.mean(centered * centered, -1, keepdims=True) + EPS)
    return centered * inverse, inverse


def norm_backward(gradient, normed, inverse, gain):
    scaled = gradient * gain
    return inverse * (
        scaled
        - jnp.mean(scaled, -1, keepdims=True)
        - normed * jnp.mean(scaled * normed, -1, keepdims=True)
    )


def place(device):
    return device // DEV_CLIP, (device % DEV_CLIP) // CORES, device % CORES


def flipped(number, by):
    low, high = number % 2, number // 2
    if by & 1:
        low = 1 - low
    if by & 2:
        high = 1 - high
    return high * 2 + low


SEMS = 160
LOCAL_SEMS = 40


def block_kernel(fused, planes, micro, tok, width, ff_own, share, ff_share, *refs):
    names = ["x", "dy", "lengths", "vec", "wq", "we", "wo", "ws"]
    names += ["bo", "ig", "vo", "gq", "ge", "go", "gs"]
    if fused:
        names += ["Lq", "Le", "Lo", "Ls", "Zq", "Ze", "Zo", "Zs"]
    names += ["Wq", "We", "Wo", "Ws", "xg", "dyg", "a2g", "drg", "act", "dhid"]
    names += ["q", "kv", "mixed", "lse", "dmix", "dq", "dl"]
    names += ["sb", "sbo", "rb", "rbo", "resid", "dresid", "vfin", "be", "bq", "vexp", "vqkv", "vrow"]
    if fused:
        names += ["so", "oo", "ao", "aq", "ae", "alq", "ale", "v1", "v2", "vz", "vp", "vs", "u0", "u1", "u2", "uz", "up", "us"]
    names += ["ssem", "rsem", "lsem"]
    r = dict(zip(names, refs, strict=True))
    r["dqkv"] = r["dhid"].at[:, :, 0:QKV_WIDTH]
    me = lax.axis_index("fsdp")
    c, k, e = place(me)
    rows = CHIPS * tok

    def chip_peer(by):
        return c * DEV_CLIP + flipped(k, by) * CORES + e

    sibling = c * DEV_CLIP + k * CORES + (1 - e)

    def plane_peer(by):
        return flipped(c, by) * DEV_CLIP + k * CORES + e

    counters = {"remote": 0, "local": 0}
    pending = []

    def send(src, dst, device):
        i = counters["remote"]
        counters["remote"] += 1
        copy = pltpu.make_async_remote_copy(
            src_ref=src, dst_ref=dst, send_sem=r["ssem"].at[i], recv_sem=r["rsem"].at[i],
            device_id=(device,), device_id_type=pl.DeviceIdType.MESH,
        )
        copy.start()
        state = {"sent": False}

        def wait_send():
            if not state["sent"]:
                state["sent"] = True
                copy.wait_send()

        copy_handle = (copy.wait_recv, wait_send)
        pending.append(wait_send)
        return copy_handle

    def local(src, dst):
        i = counters["local"]
        counters["local"] += 1
        copy = pltpu.make_async_copy(src, dst, r["lsem"].at[i])
        copy.start()
        return copy.wait

    def recv_all(handles):
        for handle in handles:
            handle[0]()

    def sent_all(handles):
        for handle in handles:
            handle[1]()

    peers = [chip_peer(by) for by in (1, 2, 3)] + [sibling]
    if fused:
        peers += [plane_peer(by) for by in range(1, planes)]
    barrier = pltpu.get_barrier_semaphore()
    for peer in peers:
        pl.semaphore_signal(barrier, inc=1, device_id=(peer,), device_id_type=pl.DeviceIdType.MESH)
    pl.semaphore_wait(barrier, len(peers))

    Wq, We, Wo, Ws = r["Wq"], r["We"], r["Wo"], r["Ws"]
    Ws2 = Ws.reshape(ff_own, width)
    flat = {name: r[name].reshape(micro * rows, width) for name in ("act", "dhid", "drg", "a2g", "dyg", "xg", "sbo")}
    chip_rows = CHIPS * share
    plane_rows = CORES * chip_rows

    def stacked(name, count, lanes):
        return flat[name].at[0:count * chip_rows].reshape(count, chip_rows, width).at[:, :, 0:lanes]

    def by_core(own, other):
        return jnp.where(e == 0, own, other), jnp.where(e == 0, other, own)

    def join_rows(own, other, count):
        first, second = by_core(own, other)
        pieces = []
        for j in range(count):
            pieces += [first[j * share:(j + 1) * share], second[j * share:(j + 1) * share]]
        return jnp.concatenate(pieces, 0)

    def split_rows(block, count):
        pieces = [block[j * share:(j + 1) * share] for j in range(2 * count)]
        return by_core(jnp.concatenate(pieces[0::2], 0), jnp.concatenate(pieces[1::2], 0))

    def join_planes(own, other, out):
        @pl.loop(0, planes)
        def _(i):
            block = join_rows(own[i].astype(F32), other[i].astype(F32), CHIPS)
            out[pl.ds(pl.multiple_of(i * plane_rows, plane_rows), plane_rows), :] = block.astype(BF)

    def split_planes(grads, own, other):
        @pl.loop(0, planes)
        def _(i):
            block = grads[pl.ds(pl.multiple_of(i * plane_rows, plane_rows), plane_rows), :].astype(F32)
            mine, theirs = split_rows(block, CHIPS)
            own[i] = mine.astype(BF)
            other[i] = theirs.astype(BF)

    def gather_start(src, dst, b):
        return [send(src, dst.at[b, k], chip_peer(by)) for by in (3, 1, 2)]

    x_local = [local(r["x"].at[b], r["xg"].at[b, k]) for b in range(micro)]
    dy_local = [local(r["dy"].at[b], r["dyg"].at[b, k]) for b in range(micro)]
    x_gather = [None] * micro
    dy_gather = [None] * micro
    if fused:
        wq_own = local(r["wq"].at[k], r["alq"].at[k])
        we_own = local(r["we"].at[k], r["ale"].at[k])
        wo_own = local(r["wo"], r["so"].at[c])
        ws_own = local(r["ws"], Ws.at[c, e])
        wq_plane = [send(r["wq"].at[flipped(k, by)], r["alq"].at[k], chip_peer(by)) for by in (3, 1, 2)]
        vec_z = [send(r["vec"], r["vz"].at[by - 1], plane_peer(by)) for by in range(1, planes)]
        x_gather[0] = gather_start(r["x"].at[0], r["xg"], 0)
        recv_all(wq_plane)
        wq_own()
        wq_mine, wq_other = stacked("drg", planes, QKV_WIDTH), stacked("a2g", planes, QKV_WIDTH)
        we_mine, we_other = stacked("act", planes, ff_own), stacked("dhid", planes, ff_own)

        def pack_plane(blocks, out):
            out[c] = jnp.concatenate([blocks[j].astype(F32) for j in range(CHIPS)], 0).astype(BF)

        pack_plane(r["alq"], wq_mine)
        wq_z = [send(wq_mine.at[c], wq_mine.at[c], plane_peer(by)) for by in range(1, planes)]
        wo_z = [send(r["wo"], r["so"].at[c], plane_peer(by)) for by in range(1, planes)]
        we_plane = [send(r["we"].at[flipped(k, by)], r["ale"].at[k], chip_peer(by)) for by in (3, 1, 2)]
        recv_all(vec_z)
        total = r["vec"][...]
        for by in range(1, planes):
            total = total + r["vz"][by - 1]
        r["v1"][...] = total
        vec_p = [send(r["v1"], r["vp"].at[by - 1], chip_peer(by)) for by in (1, 2, 3)]
        for b in range(1, micro):
            x_gather[b] = gather_start(r["x"].at[b], r["xg"], b)
        recv_all(vec_p)
        total = r["v1"][...]
        for by in (1, 2, 3):
            total = total + r["vp"][by - 1]
        r["v2"][...] = total
        vec_s = [send(r["v2"], r["vs"], sibling)]
        recv_all(we_plane)
        we_own()
        wo_own()
        ws_own()
        pack_plane(r["ale"], we_mine)
        we_z = [send(we_mine.at[c], we_mine.at[c], plane_peer(by)) for by in range(1, planes)]
        ws_z = [send(r["ws"], Ws.at[c, e], plane_peer(by)) for by in range(1, planes)]
        recv_all(vec_s)
        r["vfin"][...] = r["v2"][...] + r["vs"][...]
    else:
        loads = [local(r["wq"], Wq), local(r["we"], We), local(r["wo"], Wo), local(r["ws"], Ws2)]
        for b in range(micro):
            x_gather[b] = gather_start(r["x"].at[b], r["xg"], b)
        r["vfin"][...] = r["vec"][...]
        for load in loads:
            load()
    for b in range(micro):
        dy_gather[b] = gather_start(r["dy"].at[b], r["dyg"], b)

    vfin = r["vfin"]
    own_row = lax.broadcasted_iota(jnp.int32, (CHIPS, width), 0) == k
    r["be"][...] = jnp.sum(jnp.where(own_row, vfin[ROW_EXPAND:ROW_EXPAND + CHIPS, :], 0.0), 0, keepdims=True)
    r["bq"][...] = jnp.sum(jnp.where(own_row, vfin[ROW_QKV:ROW_QKV + CHIPS, :], 0.0), 0, keepdims=True)[:, :QKV_WIDTH]
    r["vrow"][...] = jnp.zeros_like(r["vrow"])
    r["vexp"][...] = jnp.zeros_like(r["vexp"])
    r["vqkv"][...] = jnp.zeros_like(r["vqkv"])

    def vec_row(index):
        return vfin[index:index + 1, :]

    def add_row(index, value):
        r["vrow"][index:index + 1, :] += value

    for b in range(micro):
        x_local[b]()
        recv_all(x_gather[b])

        @pl.loop(0, CHIPS)
        def _(i):
            normed, _inverse = norm_parts(r["xg"][b, i].astype(F32))
            r["xg"][b, i] = (normed * vec_row(ROW_GAIN_ONE) + vec_row(ROW_SHIFT_ONE)).astype(BF)

    if fused:
        recv_all(wq_z)
        wq_s = [send(wq_mine, wq_other, sibling)]
        recv_all(wo_z)
        wo_s = [send(r["so"], r["oo"], sibling)]
        recv_all(wq_s)
        join_planes(wq_mine, wq_other, Wq)

    kv_swap = [None] * micro
    half = rows // 2
    for b in range(micro):

        @pl.loop(0, 2)
        def _(i):
            lines = r["xg"].reshape(micro, rows, width)[b, pl.ds(pl.multiple_of(i * half, half), half), :]
            out = (dot_nn(lines, Wq[...]) + r["bq"][...]).astype(BF)
            at = pl.ds(pl.multiple_of(i * half, half), half)
            for h in range(OWN_HEADS):
                r["q"][b, h, at, :] = out[:, h * HD:(h + 1) * HD]
                for part in range(2):
                    low = (part + 1) * OWN_FEATURES + h * HD
                    r["kv"][b, part, h, e, at, :] = out[:, low:low + HD]

        kv_swap[b] = [send(r["kv"].at[b, :, :, e], r["kv"].at[b, :, :, e], sibling)]

    keys = CORES * rows
    chunk_places = [(2 * (i % CHIPS) + i // CHIPS) * tok for i in range(DEV_CLIP)]

    def masked_scores(b, key_rows, query_rows):
        raw = dot_nt(key_rows, query_rows)
        index = lax.broadcasted_iota(jnp.int32, (tok, raw.shape[1]), 0)
        length = r["lengths"][b, c]
        return jnp.concatenate(
            [
                jnp.where(index < length - first, raw[i * tok:(i + 1) * tok] * SCALE, NEG)
                for i, first in enumerate(chunk_places)
            ],
            0,
        )

    def attend(b):
        @pl.loop(0, OWN_HEADS * 2)
        def _(step):
            h, part = step // 2, step % 2
            at = pl.ds(pl.multiple_of(part * half, half), half)
            key_rows = r["kv"][b, 0, h].reshape(keys, HD)
            value_rows = r["kv"][b, 1, h].reshape(keys, HD)
            scores = masked_scores(b, key_rows, r["q"][b, h, at, :])
            peak = jnp.max(scores, 0, keepdims=True)
            exponent = jnp.exp(scores - peak)
            sums = jnp.sum(exponent, 0, keepdims=True)
            probs = (exponent * (1.0 / sums)).astype(BF)
            r["lse"][b, h, :, at] = peak + jnp.log(sums)
            r["mixed"][b, h, :, at] = dot_tn(value_rows, probs).astype(BF)

    def reduce_start(slots, landing, b):
        return [send(slots.at[b, flipped(k, by)], landing.at[b, by - 1], chip_peer(by)) for by in (3, 1, 2)]

    def reduced(slots, landing, b):
        total = slots[b, k].astype(F32)
        for by in (1, 2, 3):
            total = total + landing[b, by - 1].astype(F32)
        return total

    def tiles(count, body):
        @pl.loop(0, count)
        def _(i):
            body(pl.ds(pl.multiple_of(i * TILE, TILE), TILE))

    def partial_sum(slots, b, product):
        view = slots.reshape(micro, rows, width)

        def body(at):
            view[b, :, at] = product(at).astype(BF)

        tiles(width // TILE, body)

    sb, sbo, rb, rbo = r["sb"], r["sbo"], r["rb"], r["rbo"]
    first_reduce = [None] * micro
    for b in range(micro):
        recv_all(kv_swap[b])
        attend(b)
        if fused and b == 0:
            recv_all(wo_s)
            for i in range(planes):
                pair = join_rows(r["so"][i].astype(F32), r["oo"][i].astype(F32), 1)
                Wo[i * HD:(i + 1) * HD, :] = pair.astype(BF)
        lines = r["mixed"].reshape(micro, OWN_FEATURES, rows)
        partial_sum(sb, b, lambda at: dot_tn(lines[b], Wo[:, at]))
        first_reduce[b] = reduce_start(sb, rb, b)

    second_gather = [None] * micro
    for b in range(micro):
        recv_all(first_reduce[b])
        residual = r["x"][b].astype(F32) + reduced(sb, rb, b) + vec_row(ROW_BIAS_OUT)
        r["resid"][b] = residual
        normed, _inverse = norm_parts(residual)
        r["a2g"][b, k] = (normed * vec_row(ROW_GAIN_TWO) + vec_row(ROW_SHIFT_TWO)).astype(BF)
        second_gather[b] = gather_start(r["a2g"].at[b, k], r["a2g"], b)

    if fused:
        recv_all(we_z)
        we_s = [send(we_mine, we_other, sibling)]
        recv_all(ws_z)
        ws_s = [send(Ws.at[:, e], Ws.at[:, e], sibling)]
        recv_all(we_s)
        sent_all(we_s + we_z + wq_s + wq_z)
        join_planes(we_mine, we_other, We)
        recv_all(ws_s)

    a2_rows = r["a2g"].reshape(micro, rows, width)
    dy_rows = r["dyg"].reshape(micro, rows, width)
    dr_rows = r["drg"].reshape(micro, rows, width)
    a1_rows = r["xg"].reshape(micro, rows, width)
    hidden_reduce = [None] * micro
    for b in range(micro):
        recv_all(second_gather[b])
        dy_local[b]()
        recv_all(dy_gather[b])

        def feed(at):
            hidden = dot_nn(a2_rows[b], We[:, at]) + r["be"][:, at]
            grad_active = dot_nt(dy_rows[b], Ws2[at, :]).astype(BF).astype(F32)
            normal = 0.5 * (1.0 + lax.erf(hidden * 0.7071067811865476))
            r["act"][b, :, at] = (hidden * normal).astype(BF)
            density = jnp.exp(-0.5 * hidden * hidden) * 0.3989422804014327
            grad_hidden = (grad_active * (normal + hidden * density)).astype(BF)
            r["dhid"][b, :, at] = grad_hidden
            r["vexp"][:, at] += jnp.sum(grad_hidden.astype(F32), 0, keepdims=True)

        tiles(ff_own // TILE, feed)
        sent_all(first_reduce[b])
        partial_sum(sb, b, lambda at: dot_nt(r["dhid"][b], We[at, :]))
        hidden_reduce[b] = reduce_start(sb, rb, b)

    def finish_hidden(b):
        recv_all(hidden_reduce[b])
        gradient = reduced(sb, rb, b)
        normed, inverse = norm_parts(r["resid"][b])
        dy_own = r["dy"][b].astype(F32)
        total = dy_own + norm_backward(gradient, normed, inverse, vec_row(ROW_GAIN_TWO))
        r["dresid"][b] = total
        r["drg"][b, k] = total.astype(BF)
        gathers = gather_start(r["drg"].at[b, k], r["drg"], b)
        add_row(ROW_GAIN_TWO, jnp.sum(gradient * normed, 0, keepdims=True))
        add_row(ROW_SHIFT_TWO, jnp.sum(gradient, 0, keepdims=True))
        add_row(ROW_BIAS_OUT, jnp.sum(total, 0, keepdims=True))
        add_row(ROW_BIAS_SHRINK, jnp.sum(dy_own, 0, keepdims=True))
        return gathers

    resid_gather = [None] * micro
    out_reduce = [None] * micro
    for b in range(micro):
        partial_sum(sbo, b, lambda at: dot_nn(r["act"][b], Ws2[:, at]))
        resid_gather[b] = finish_hidden(b)
        out_reduce[b] = reduce_start(sbo, rbo, b)

    def weight_gradient(count, lefts, rights, out):
        def body(at):
            total = dot_tn(lefts[0, :, at], rights[0])
            for b in range(1, micro):
                total = total + dot_tn(lefts[b, :, at], rights[b])
            out[at, :] = total.astype(BF)

        tiles(count // TILE, body)

    if fused:
        sent_all(ws_z + ws_s + wo_z + wo_s + wq_plane + we_plane)

    def sibling_add(handles, landing, fetched, out, mine):
        recv_all(handles)
        sent_all(handles)
        local(landing, fetched)()

        @pl.loop(0, planes)
        def _(i):
            out[i] = (mine(i).astype(F32) + fetched[i].astype(F32)).astype(BF)

    def plane_start(space, landing):
        return [send(space.at[flipped(c, by)], landing.at[by - 1], plane_peer(by)) for by in range(1, planes)]

    def plane_sum(handles, space, landing, arrived):
        recv_all(handles)
        local(landing, arrived)()
        total = space[c].astype(F32)
        for by in range(1, planes):
            total = total + arrived[by - 1].astype(F32)
        return total

    weight_gradient(ff_own, r["act"], dy_rows, Ws2)
    if fused:
        gs_s = [send(Ws.at[:, 1 - e], r["Ls"], sibling)]
    weight_gradient(width, a2_rows, r["dhid"], We)
    if fused:
        space_e, other_e = stacked("act", planes, ff_own), stacked("dhid", planes, ff_own)
        split_planes(We, space_e, other_e)
        ge_s = [send(other_e, r["Le"], sibling)]
        sent_all(second_gather[0] + second_gather[1] + dy_gather[0] + dy_gather[1])
        space_s = flat["dyg"].at[0:planes * ff_share].reshape(planes, ff_share, width)
        arrived_s = flat["a2g"].at[0:(planes - 1) * ff_share].reshape(planes - 1, ff_share, width)
        arrived_e = flat["a2g"].at[512:512 + (planes - 1) * chip_rows].reshape(planes - 1, chip_rows, width)
        sibling_add(gs_s, r["Ls"], space_s, space_s, lambda i: Ws[i, e])
        gs_z = plane_start(space_s, r["Zs"])
        sibling_add(ge_s, r["Le"], other_e, space_e, lambda i: space_e[i])
        ge_z = plane_start(space_e, r["Ze"])

    def mixed_gradient(b):
        recv_all(resid_gather[b])

        @pl.loop(0, 2)
        def _(i):
            at = pl.ds(pl.multiple_of(i * half, half), half)
            out = dot_nt(dr_rows[b, at, :], Wo[...]).astype(BF)
            for h in range(OWN_HEADS):
                r["dmix"][h, at, :] = out[:, h * HD:(h + 1) * HD]

    def attend_back(b):
        sent_all(kv_swap[b])

        @pl.loop(0, OWN_HEADS)
        def _(h):
            key_rows = r["kv"][b, 0, h].reshape(keys, HD)
            value_rows = r["kv"][b, 1, h].reshape(keys, HD)
            grad_keys = None
            grad_values = None
            for part in range(2):
                at = pl.ds(part * half, half)
                query_rows = r["q"][b, h, at, :]
                mix_rows = r["dmix"][h, at, :]
                probs = jnp.exp(masked_scores(b, key_rows, query_rows) - r["lse"][b, h, :, at])
                grad_probs = dot_nt(value_rows, mix_rows)
                inner = jnp.sum(probs * grad_probs, 0, keepdims=True)
                grad_scores = (probs * (grad_probs - inner)).astype(BF)
                grad_query = dot_tn(key_rows, grad_scores) * SCALE
                r["dq"][h, at, :] = grad_query.T.astype(BF)
                key_term = dot_nn(grad_scores, query_rows)
                value_term = dot_nn(probs.astype(BF), mix_rows)
                grad_keys = key_term if grad_keys is None else grad_keys + key_term
                grad_values = value_term if grad_values is None else grad_values + value_term
            r["kv"][b, 0, h] = (grad_keys * SCALE).astype(BF).reshape(CORES, rows, HD)
            r["kv"][b, 1, h] = grad_values.astype(BF).reshape(CORES, rows, HD)

        return [send(r["kv"].at[b, :, :, 1 - e], r["dl"].at[b], sibling)]

    def join_gradients(b, handles):
        recv_all(handles)

        @pl.loop(0, CHIPS)
        def _(i):
            at = pl.ds(pl.multiple_of(i * tok, tok), tok)
            pieces = [r["dq"][h, at, :] for h in range(OWN_HEADS)]
            for part in range(2):
                for h in range(OWN_HEADS):
                    pair = r["kv"][b, part, h, e, at, :].astype(F32) + r["dl"][b, part, h, at, :].astype(F32)
                    pieces.append(pair.astype(BF))
            pieces.append(jnp.zeros((tok, QKV_WIDTH - 3 * OWN_FEATURES), BF))
            line = jnp.concatenate(pieces, 1)
            r["dqkv"][b, at, :] = line
            r["vqkv"][...] += jnp.sum(line.astype(F32), 0, keepdims=True)

    def input_start(b):
        sent_all(hidden_reduce[b])
        partial_sum(sb, b, lambda at: dot_nt(r["dqkv"][b], Wq[at, :]))
        return reduce_start(sb, rb, b)

    def finish_input(b, handles):
        recv_all(handles)
        gradient = reduced(sb, rb, b)
        normed, inverse = norm_parts(r["x"][b].astype(F32))
        back = norm_backward(gradient, normed, inverse, vec_row(ROW_GAIN_ONE))
        r["ig"][b] = (r["dresid"][b] + back).astype(BF)
        add_row(ROW_GAIN_ONE, jnp.sum(gradient * normed, 0, keepdims=True))
        add_row(ROW_SHIFT_ONE, jnp.sum(gradient, 0, keepdims=True))

    def finish_out(b):
        recv_all(out_reduce[b])
        total = r["resid"][b] + reduced(sbo, rbo, b) + vec_row(ROW_BIAS_SHRINK)
        r["bo"][b] = total.astype(BF)

    input_reduce = [None] * micro
    swap = None
    for b in range(micro):
        mixed_gradient(b)
        if b == micro - 1:
            mixed2 = r["mixed"].reshape(micro, OWN_FEATURES, rows)
            lead = dot_nn(mixed2[0], dr_rows[0])
            for other in range(1, micro):
                lead = lead + dot_nn(mixed2[other], dr_rows[other])
            if fused:
                space_o, other_o, arrived_o = r["so"], r["oo"], r["ao"]
                for i in range(planes):
                    mine, theirs = split_rows(lead[i * HD:(i + 1) * HD], 1)
                    space_o[i] = mine.astype(BF)
                    other_o[i] = theirs.astype(BF)
                go_s = [send(other_o, r["Lo"], sibling)]
            else:
                Wo[...] = lead.astype(BF)
        if b > 0:
            join_gradients(b - 1, swap)
            input_reduce[b - 1] = input_start(b - 1)
        swap = attend_back(b)
    last = micro - 1
    join_gradients(last, swap)
    input_reduce[last] = input_start(last)
    weight_gradient(width, a1_rows, r["dqkv"], Wq)
    if fused:
        sent_all(resid_gather[0] + resid_gather[1])
        space_q, other_q = stacked("drg", planes, QKV_WIDTH), stacked("xg", planes, QKV_WIDTH)
        arrived_q = stacked("sbo", planes - 1, QKV_WIDTH)
        split_planes(Wq, space_q, other_q)
        gq_s = [send(other_q, r["Lq"], sibling)]
        sibling_add(go_s, r["Lo"], other_o, space_o, lambda i: space_o[i])
        go_z = plane_start(space_o, r["Zo"])
        sibling_add(gq_s, r["Lq"], other_q, space_q, lambda i: space_q[i])
        gq_z = plane_start(space_q, r["Zq"])
        sent_all(out_reduce[0] + out_reduce[1])
    for b in range(micro):
        finish_out(b)
    for b in range(micro):
        finish_input(b, input_reduce[b])

    mine_e = lax.broadcasted_iota(jnp.int32, (VEC_ROWS, width), 0) == ROW_EXPAND + k
    mine_q = lax.broadcasted_iota(jnp.int32, (VEC_ROWS, width), 0) == ROW_QKV + k
    padded = jnp.concatenate([r["vqkv"][...], jnp.zeros((1, width - QKV_WIDTH), F32)], 1)
    sums = r["vrow"][...] + jnp.where(mine_e, r["vexp"][...], 0.0) + jnp.where(mine_q, padded, 0.0)
    if fused:
        r["u0"][...] = sums

        def unpack_plane(total, blocks):
            for j in range(CHIPS):
                blocks[j] = total[j * share:(j + 1) * share].astype(BF)

        sum_z = [send(r["u0"], r["uz"].at[by - 1], plane_peer(by)) for by in range(1, planes)]
        r["gs"][...] = plane_sum(gs_z, space_s, r["Zs"], arrived_s)
        recv_all(sum_z)
        total = r["u0"][...]
        for by in range(1, planes):
            total = total + r["uz"][by - 1]
        r["u1"][...] = total
        sum_p = [send(r["u1"], r["up"].at[by - 1], chip_peer(by)) for by in (1, 2, 3)]
        unpack_plane(plane_sum(ge_z, space_e, r["Ze"], arrived_e), r["ae"])
        ge_p = [send(r["ae"].at[flipped(k, by)], r["ale"].at[k], chip_peer(by)) for by in (3, 1, 2)]
        recv_all(sum_p)
        total = r["u1"][...]
        for by in (1, 2, 3):
            total = total + r["up"][by - 1]
        r["u2"][...] = total
        sum_s = [send(r["u2"], r["us"], sibling)]
        unpack_plane(plane_sum(gq_z, space_q, r["Zq"], arrived_q), r["aq"])
        gq_p = [send(r["aq"].at[flipped(k, by)], r["alq"].at[k], chip_peer(by)) for by in (3, 1, 2)]
        r["go"][...] = plane_sum(go_z, space_o, r["Zo"], arrived_o)
        recv_all(sum_s)
        r["vo"][...] = r["u2"][...] + r["us"][...]
        recv_all(ge_p)
        r["ge"][k] = r["ae"][k].astype(F32)
        for by in (1, 2, 3):
            r["ge"][flipped(k, by)] = r["ale"][flipped(k, by)].astype(F32)
        recv_all(gq_p)
        r["gq"][k] = r["aq"][k].astype(F32)
        for by in (1, 2, 3):
            r["gq"][flipped(k, by)] = r["alq"][flipped(k, by)].astype(F32)
    else:
        r["vo"][...] = sums
        stores = [local(Wq, r["gq"]), local(We, r["ge"]), local(Wo, r["go"]), local(Ws2, r["gs"])]
        for store in stores:
            store()
    for wait in pending:
        wait()


def run_block(fused, planes, x, dy, lengths, vec, wq, we, wo, ws, share, ff_share):
    micro, tok, width = x.shape
    ff_own = width
    rows = CHIPS * tok
    vmem = pl.BlockSpec(memory_space=pltpu.VMEM)
    anywhere = pl.BlockSpec(memory_space=pl.ANY)
    smem = pl.BlockSpec(memory_space=pltpu.SMEM)

    def shape(*dims, dtype=BF):
        return jax.ShapeDtypeStruct(dims, dtype)

    outs = [
        (shape(micro, tok, width), vmem),
        (shape(micro, tok, width), vmem),
        (shape(VEC_ROWS, width, dtype=F32), vmem),
    ]
    if fused:
        outs += [
            (shape(CHIPS, share, QKV_WIDTH, dtype=F32), vmem),
            (shape(CHIPS, share, ff_own, dtype=F32), vmem),
            (shape(share, width, dtype=F32), vmem),
            (shape(ff_share, width, dtype=F32), vmem),
        ]
        for count in (planes, planes - 1):
            outs += [
                (shape(count, CHIPS * share, QKV_WIDTH), anywhere),
                (shape(count, CHIPS * share, ff_own), anywhere),
                (shape(count, share, width), anywhere),
                (shape(count, ff_share, width), anywhere),
            ]
    else:
        outs += [
            (shape(width, QKV_WIDTH), anywhere),
            (shape(width, ff_own), anywhere),
            (shape(OWN_FEATURES, width), anywhere),
            (shape(ff_own, width), anywhere),
        ]
    if fused:
        weights = [
            pltpu.VMEM((width, QKV_WIDTH), BF),
            pltpu.VMEM((width, ff_own), BF),
            pltpu.VMEM((OWN_FEATURES, width), BF),
            pltpu.VMEM((planes, CORES, ff_share, width), BF),
        ]
    else:
        weights = [
            pltpu.VMEM((width, QKV_WIDTH), BF),
            pltpu.VMEM((width, ff_own), BF),
            pltpu.VMEM((OWN_FEATURES, width), BF),
            pltpu.VMEM((ff_own, width), BF),
        ]
    scratch = weights + [
        pltpu.VMEM((micro, CHIPS, tok, width), BF),
        pltpu.VMEM((micro, CHIPS, tok, width), BF),
        pltpu.VMEM((micro, CHIPS, tok, width), BF),
        pltpu.VMEM((micro, CHIPS, tok, width), BF),
        pltpu.VMEM((micro, rows, ff_own), BF),
        pltpu.VMEM((micro, rows, ff_own), BF),
        pltpu.VMEM((micro, OWN_HEADS, rows, HD), BF),
        pltpu.VMEM((micro, 2, OWN_HEADS, CORES, rows, HD), BF),
        pltpu.VMEM((micro, OWN_HEADS, HD, rows), BF),
        pltpu.VMEM((micro, OWN_HEADS, 1, rows), F32),
        pltpu.VMEM((OWN_HEADS, rows, HD), BF),
        pltpu.VMEM((OWN_HEADS, rows, HD), BF),
        pltpu.VMEM((micro, 2, OWN_HEADS, rows, HD), BF),
        pltpu.VMEM((micro, CHIPS, tok, width), BF),
        pltpu.VMEM((micro, CHIPS, tok, width), BF),
        pltpu.VMEM((micro, CHIPS - 1, tok, width), BF),
        pltpu.VMEM((micro, CHIPS - 1, tok, width), BF),
        pltpu.VMEM((micro, tok, width), F32),
        pltpu.VMEM((micro, tok, width), F32),
        pltpu.VMEM((VEC_ROWS, width), F32),
        pltpu.VMEM((1, ff_own), F32),
        pltpu.VMEM((1, QKV_WIDTH), F32),
        pltpu.VMEM((1, ff_own), F32),
        pltpu.VMEM((1, QKV_WIDTH), F32),
        pltpu.VMEM((VEC_ROWS, width), F32),
    ]
    if fused:
        scratch += [
            pltpu.VMEM((planes, share, width), BF),
            pltpu.VMEM((planes, share, width), BF),
            pltpu.VMEM((planes - 1, share, width), BF),
            pltpu.VMEM((CHIPS, share, QKV_WIDTH), BF),
            pltpu.VMEM((CHIPS, share, ff_own), BF),
            pltpu.VMEM((CHIPS, share, QKV_WIDTH), BF),
            pltpu.VMEM((CHIPS, share, ff_own), BF),
        ]
        for _ in range(2):
            if _ == 1:
                scratch.append(pltpu.VMEM((VEC_ROWS, width), F32))
            scratch += [
                pltpu.VMEM((VEC_ROWS, width), F32),
                pltpu.VMEM((VEC_ROWS, width), F32),
                pltpu.VMEM((planes - 1, VEC_ROWS, width), F32),
                pltpu.VMEM((CHIPS - 1, VEC_ROWS, width), F32),
                pltpu.VMEM((VEC_ROWS, width), F32),
            ]
    scratch += [
        pltpu.SemaphoreType.DMA((SEMS,)),
        pltpu.SemaphoreType.DMA((SEMS,)),
        pltpu.SemaphoreType.DMA((LOCAL_SEMS,)),
    ]
    return pl.pallas_call(
        partial(block_kernel, fused, planes, micro, tok, width, ff_own, share, ff_share),
        out_shape=[out for out, _ in outs],
        in_specs=[vmem, vmem, smem, vmem, anywhere, anywhere, anywhere, anywhere],
        out_specs=[spec for _, spec in outs],
        scratch_shapes=scratch,
        compiler_params=pltpu.CompilerParams(
            collective_id=0, has_side_effects=True, vmem_limit_bytes=63 * 1000 * 1000
        ),
    )(x, dy, lengths, vec, wq, we, wo, ws)


def by_chip(matrix, part):
    rows = matrix.shape[0]
    return matrix.reshape(rows, -1, CHIPS, part).transpose(2, 0, 1, 3).reshape(CHIPS, rows, -1)


def from_chips(blocks, part):
    rows = blocks.shape[1]
    return blocks.reshape(CHIPS, rows, -1, part).transpose(1, 2, 0, 3).reshape(rows, -1)


def body(
    inputs, cotangent, lengths, first_gain, first_shift, query_weight, query_bias, key_weight,
    value_weight, value_bias, output_weight, output_bias, second_gain, second_shift,
    expand_weight, expand_bias, shrink_weight, shrink_bias,
):
    device = lax.axis_index("fsdp")
    count = lax.axis_size("fsdp")
    c, k, e = place(device)
    planes = count // DEV_CLIP
    width = inputs.shape[2]
    share = query_weight.shape[0]
    ff_share = shrink_weight.shape[0]
    ff_part = width // 4
    fused = planes == 4 and share * 2 == HD and ff_share * 2 == ff_part
    plain = (first_gain, first_shift, second_gain, second_shift, output_bias, shrink_bias)
    low = [w.astype(BF) for w in (query_weight, key_weight, value_weight, expand_weight, output_weight, shrink_weight)]
    if fused:
        vec = jnp.zeros((VEC_ROWS, width), F32)
        vec = lax.dynamic_update_slice(vec, jnp.stack(plain), (0, device * share))
        vec = lax.dynamic_update_slice(vec, expand_bias[None], (ROW_EXPAND + k, (2 * c + e) * ff_share))
        at = (2 * c + e) * share
        vec = lax.dynamic_update_slice(vec, query_bias[None], (ROW_QKV + k, at))
        vec = lax.dynamic_update_slice(vec, value_bias[None], (ROW_QKV + k, 2 * OWN_FEATURES + at))
        wide = [by_chip(w, HD) for w in low[:3]]
        wide.append(jnp.zeros((CHIPS, share, QKV_WIDTH - 3 * OWN_FEATURES), BF))
        wq = jnp.concatenate(wide, 2)
        we = by_chip(low[3], ff_part)
        got = run_block(True, planes, inputs, cotangent, lengths, vec, wq, we, low[4], low[5], share, ff_share)
        block_out, input_grad, sums, gq, ge, grad_output_w, grad_shrink_w = got[:7]
        grad_query_w, grad_key_w, grad_value_w = (
            from_chips(gq[:, :, i * OWN_FEATURES:(i + 1) * OWN_FEATURES], HD) for i in range(3)
        )
        grad_expand_w = from_chips(ge, ff_part)
        own = lax.dynamic_slice(sums, (0, device * share), (len(plain), share))
        owned = [own[i] for i in range(len(plain))]
        grad_expand_b = lax.dynamic_slice(sums, (ROW_EXPAND + k, (2 * c + e) * ff_share), (1, ff_share))[0]
        grad_query_b = lax.dynamic_slice(sums, (ROW_QKV + k, at), (1, share))[0]
        grad_value_b = lax.dynamic_slice(sums, (ROW_QKV + k, 2 * OWN_FEATURES + at), (1, share))[0]
    else:

        def whole(array):
            return lax.all_gather(array, "fsdp", axis=0, tiled=True)

        def mine(blocks):
            return lax.dynamic_index_in_dim(blocks, k, 0, keepdims=False)

        full = [whole(w) for w in low]
        pieces = [mine(by_chip(w, HD)) for w in full[:3]]
        pieces.append(jnp.zeros((width, QKV_WIDTH - 3 * OWN_FEATURES), BF))
        wq = jnp.concatenate(pieces, 1)
        we = mine(by_chip(full[3], ff_part))
        wo = mine(by_chip(full[4].T, HD)).T
        ws = mine(by_chip(full[5].T, ff_part)).T
        blank = jnp.zeros((2, width), F32)
        bias_e = by_chip(whole(expand_bias)[None], ff_part)[:, 0]
        bias_q = by_chip(whole(query_bias)[None], HD)[:, 0]
        bias_v = by_chip(whole(value_bias)[None], HD)[:, 0]
        bias_rows = jnp.concatenate(
            [bias_q, jnp.zeros_like(bias_q), bias_v, jnp.zeros((CHIPS, width - 3 * OWN_FEATURES), F32)], 1
        )
        vec = jnp.concatenate([jnp.stack([whole(v) for v in plain]), blank, bias_e, bias_rows])
        got = run_block(False, planes, inputs, cotangent, lengths, vec, wq, we, wo, ws, share, ff_share)
        block_out, input_grad, sums, gq, ge, go, gs = got[:7]

        def spread(block, part):
            places = lax.broadcasted_iota(jnp.int32, (CHIPS, 1, 1), 0) == k
            return from_chips(jnp.where(places, block.astype(F32)[None], 0.0), part)

        def owned_sum(array):
            return lax.psum_scatter(array, "fsdp", scatter_dimension=0, tiled=True)

        grad_query_w, grad_key_w, grad_value_w = (
            owned_sum(spread(gq[:, i * OWN_FEATURES:(i + 1) * OWN_FEATURES], HD)) for i in range(3)
        )
        grad_expand_w = owned_sum(spread(ge, ff_part))
        grad_output_w = owned_sum(spread(go.T, HD).T)
        grad_shrink_w = owned_sum(spread(gs.T, ff_part).T)
        owned = [owned_sum(sums[i]) for i in range(len(plain))]
        sums_q = sums[ROW_QKV:ROW_QKV + CHIPS, None]
        grad_expand_b = owned_sum(from_chips(sums[ROW_EXPAND:ROW_EXPAND + CHIPS, None], ff_part)[0])
        grad_query_b = owned_sum(from_chips(sums_q[:, :, :OWN_FEATURES], HD)[0])
        grad_value_b = owned_sum(from_chips(sums_q[:, :, 2 * OWN_FEATURES:3 * OWN_FEATURES], HD)[0])
    return (
        block_out,
        input_grad,
        owned[0],
        owned[1],
        grad_query_w,
        grad_query_b,
        grad_key_w,
        grad_value_w,
        grad_value_b,
        grad_output_w,
        owned[4],
        owned[2],
        owned[3],
        grad_expand_w,
        grad_expand_b,
        grad_shrink_w,
        owned[5],
    )


def solution(mesh):
    rows, matrix, vector = P(None, "fsdp", None), P("fsdp", None), P("fsdp")
    in_specs = (
        rows, rows, P(), vector, vector, matrix, vector, matrix, matrix, vector, matrix, vector,
        vector, vector, matrix, vector, matrix, vector,
    )
    out_specs = (
        rows, rows, vector, vector, matrix, vector, matrix, matrix, vector, matrix, vector,
        vector, vector, matrix, vector, matrix, vector,
    )
    return jax.shard_map(body, mesh=mesh, in_specs=in_specs, out_specs=out_specs, check_vma=False)
```

time: 2070 us -> 346 us (0.17)
  waiting for transfers between devices: 1210 us -> 0 us
  Pallas kernels: 0 us -> 318 us
  starting transfers between devices: 250 us -> 0 us
  local copies, waits for them, and re-layouts: 261 us -> 22.3 us
  matrix products: 185 us -> 0 us
  other arithmetic: 84.1 us -> 3.34 us
  blocking collectives: 44.1 us -> 0 us
    reduce_scatter x1 -> x0, waiting for transfers between devices: 659 us -> none  [body(): lax.psum_scatter(owned_terms(lax.axis_size('fsdp') * block_rows, joined,...]
    pallas_call x0 -> x1, Pallas kernels: none -> 318 us  [run_block(): pl.pallas_call(partial(block_kernel, fused, planes, micro, tok, width, ff...]
    ppermute x56 -> x0, starting transfers between devices: 250 us -> none  [shifted(): return lax.ppermute(x, axis, pairs)]
    ppermute x56 -> x0, waiting for transfers between devices: 211 us -> none  [shifted(): return lax.ppermute(x, axis, pairs)]
    all_gather x6 -> x0, waiting for transfers between devices: 201 us -> none  [the longest x1 70.8 us: body(): lax.all_gather(query_weight.astype(jnp.bfloat16), 'fsdp', axis=0, tiled=T...]
    dot_general x58 -> x0, matrix products: 185 us -> none  [the longest x12 57.2 us: times_plain(): return jnp.dot(left_rows, right_rows, preferred_element_type=jnp.float32)]
    unnamed x9 -> x0, waiting for transfers between devices: 138 us -> none
    unnamed x304 -> x26, local copies, waits for them, and re-layouts: 83.6 us -> 3.3 us
  transfers between devices with their start and end apart: 64 -> 0, of which waited for: 20 -> 0; matrix products, arithmetic and copies ran while one was open for 16% -> 0% of each run, Pallas kernels for 0% -> 0%
where the time goes in v1:
time: 346 us; the launch traced here: 345 us
  Pallas kernels  318 us (92%)
  local copies, waits for them, and re-layouts  22.3 us (6%)
    pallas_call x1, Pallas kernels, run_block(): pl.pallas_call(partial(block_kernel, fused, planes, micro, tok, width, ff...  318 us

profile of v1, /device:TPU:0, one launch (start us, length us, event | category | flops | bytes accessed | tf_op | source)
XLA Modules:
  0.0 344.9 jit_solution(2981011471737705716)
XLA Ops:
  0.7 0.0 copy-start.7
  0.7 0.0 copy-start.8
  0.8 0.1 pad.3.clone
  0.8 0.8 stack.27
  1.6 0.5 dynamic_update_slice.12
  2.2 0.9 dynamic_update_slice.13
  3.0 0.8 dynamic_update_slice.14
  3.8 0.8 dynamic_update_slice.15.refs_3_
  4.7 0.0 copy-start.6
  4.7 1.0 convert_element_type.18
  5.6 0.2 reshape.82
  5.9 0.1 copy.50
  6.0 0.1 reshape.83
  6.1 0.0 copy-done.7
  6.1 0.2 reshape.84
  6.4 0.0 copy-start.9
  6.4 0.1 copy.49
  6.5 0.0 copy-start.1
  6.5 0.1 reshape.85
  6.6 0.0 copy-done.8
  6.7 0.0 copy-done.6
  6.7 0.2 reshape.86
  6.9 0.1 copy.48
  7.0 0.1 reshape.87
  7.1 0.8 maximum_maximum_fusion.refs_4_
  8.0 0.0 copy-done.9
  8.0 0.7 convert_element_type.22.refs_6_
  8.6 0.0 copy-done.1
  8.7 0.0 copy-start.2
  8.7 0.5 reshape.88
  9.2 0.2 copy.47
  9.4 1.2 reshape.89.refs_5_
  10.6 0.0 copy-done.2
  10.6 0.8 convert_element_type.23.refs_7_
  11.4 318.3 %shard_map.305 = (bf16[2,128,1280]{2,1,0:T(8,128)(2,1)}, bf16[2,128,1280]{2,1,0:T(8,128)(2,1)}, f32[16,1280]{1,0:T(8,128)}, f32[4,40,1024]{2,1,0:T(8,128)}, f32[...) custom-call(bf16[2,128,1280]{2,1,0:T(8,128)(2,1)} %refs_0_.1, ...), custom_call_target="tpu_custom_call" | custom-call | tf_op jit(solution)/shard_map/pallas_call | solution.py:739
  329.6 1.4 dynamic_slice.15
  331.0 0.8 constant_dynamic-slice_fusion
  331.8 1.3 slice_bitcast_fusion
  333.1 1.3 fusion
  334.4 0.2 reshape.94
  334.6 0.2 copy.41
  334.8 1.0 reshape.95
  335.8 0.2 reshape.92
  336.0 0.2 copy.40
  336.2 0.0 copy-start
  336.2 1.0 reshape.93
  337.2 0.2 reshape.90
  337.4 0.2 copy.39
  337.7 1.0 reshape.91
  338.6 0.0 copy-done
  338.6 0.7 reshape.96
  339.3 0.6 copy.42
  339.9 0.0 copy-start.5
  340.0 0.0 copy-start.4
  340.0 1.7 reshape.97
  341.7 0.0 copy-done.5
  341.7 0.0 copy-start.10
  341.7 0.8 copy.59
  342.5 0.0 copy-done.4
  342.5 0.8 copy.60
  343.3 0.0 copy-done.10
  343.3 0.7 copy.61
  344.0 0.0 copy-done.3
  344.0 0.9 copy.62
  (6 shorter events, 0.1 us)
Async XLA Ops:
  0.7 5.5 %copy-start.7 = (f32[40,1280]{1,0:T(8,128)S(1)}, f32[40,1280]{1,0:T(8,128)}, u32[]{:S(2)}) copy-start(f32[40,1280]{1,0:T(8,128)} %param.25) | copy-start | bytes 614404
  0.7 5.9 %copy-start.8 = (f32[40,1280]{1,0:T(8,128)S(1)}, f32[40,1280]{1,0:T(8,128)}, u32[]{:S(2)}) copy-start(f32[40,1280]{1,0:T(8,128)} %param.26) | copy-start | bytes 614404
  4.7 2.0 copy-start.6
  6.4 1.6 copy-start.9
  6.5 2.2 copy-start.1
  8.7 1.9 copy-start.2
  336.2 2.4 copy-start
  339.9 1.7 copy-start.5
  340.0 2.5 copy-start.4
  341.7 1.7 copy-start.10
  341.7 2.4 copy-start.3
